TPU v7x, 256 devices: a whole 4x4x8 slice. The times are simulated.
256 devices in a mesh: cells: 32 (over y, x, core), genes: 8 (over z).
Axes of the slice: x: 4, y: 4, z: 8, core: 2. Of those that a mesh axis runs over, the one named last changes fastest.
Arguments:
- theta_shape: float32 [65536, 128], P(('cells', 'genes')), may hold values from 0.5 to 5
- theta_rate: float32 [65536, 128], P(('cells', 'genes')), may hold values from 8192 to 131072
- cell_activity: float32 [65536], P(('cells', 'genes')), may hold values from 1 to 10
- beta_shape: float32 [32768, 128], P(('cells', 'genes')), may hold values from 0.5 to 5
- beta_rate: float32 [32768, 128], P(('cells', 'genes')), may hold values from 4096 to 65536
- gene_activity: float32 [32768], P(('cells', 'genes')), may hold values from 1 to 10
- block_ids: int32 [8, 32, 16], P('genes', 'cells'), may hold values from 0 to 31, as said below
- live_blocks: int32 [8, 32], P('genes', 'cells'), may hold values from 2 to 16, as said below
- counts: bfloat16 [8, 16, 65536, 128], P('genes', None, 'cells'), may hold values from 0 to 15, as said below
Outputs:
- log_theta_shape: float32 [65536, 128], P(('cells', 'genes'))
- log_theta_rate: float32 [65536, 128], P(('cells', 'genes'))
- log_beta_shape: float32 [32768, 128], P(('cells', 'genes'))
- log_beta_rate: float32 [32768, 128], P(('cells', 'genes'))
Inputs may be any that keep to these rules, and one draw needn't show every extreme that they name: `block_ids`: the 16 block numbers of one cell shard in one gene group are distinct. `live_blocks`: some cell shard in some gene group has all 16 slots live in every draw. `counts`: Non-negative whole numbers; tiles of slots that are not live hold numbers too and do not count.
All inputs are finite; a program needn't handle non-finite values.
Results may differ from a plain program's by a relative error of at most 0.00074.
Values may be sent and summed in bfloat16 or wider, within the bound.
No kernel may reach another device: no remote copies, remote signals or barrier semaphores. Data moves between devices by JAX's collectives and lax.ppermute only.
A program may use at most 64 MiB of HBM per device.

v0:
```python
import jax
import jax.numpy as jnp
from jax import lax
from jax.experimental import pallas as pl
from jax.experimental.pallas import tpu as pltpu
from jax.sharding import Mesh, PartitionSpec as P

F32 = jnp.float32
BF16 = jnp.bfloat16
VMEM = pl.BlockSpec(memory_space=pltpu.VMEM)
HBM = pl.BlockSpec(memory_space=pltpu.HBM)
EXTRA = 16
CHUNK = 1024
GROUP = 4


def params(mib):
    return pltpu.CompilerParams(vmem_limit_bytes=mib * 1024 * 1024)


def digamma_series(value):
    shifted = value
    correction = jnp.zeros_like(value)
    for offset in range(6):
        correction = correction + 1.0 / shifted
        shifted = shifted + 1.0
    inverse = 1.0 / shifted
    square = inverse * inverse
    series = (
        jnp.log(shifted)
        - 0.5 * inverse
        - square * (1.0 / 12.0 - square * (1.0 / 120.0 - square * (1.0 / 252.0)))
    )
    return series - correction


def split_rows(beta, theta):
    row = lax.broadcasted_iota(jnp.int32, (EXTRA, beta.shape[1]), 0)
    block = jnp.zeros(row.shape, F32)
    for start, total in ((0, beta), (3, theta)):
        high = total.astype(BF16).astype(F32)
        middle = (total - high).astype(BF16).astype(F32)
        for index, part in enumerate((high, middle, total - high - middle)):
            block = jnp.where(row == start + index, part, block)
    return block.astype(BF16)


def row_totals(blocks):
    block = jnp.sum(blocks.astype(F32), axis=0)
    return jnp.sum(block[:3], axis=0, keepdims=True), jnp.sum(block[3:6], axis=0, keepdims=True)


def weights_kernel(ts_hbm, tr_hbm, bs_hbm, br_hbm, cell_ref, gene_ref, ts_s, tr_s, bs_s, br_s, sems):
    pairs = ((bs_hbm, bs_s), (br_hbm, br_s), (ts_hbm, ts_s), (tr_hbm, tr_s))
    moves = [pltpu.make_async_copy(*pair, sems.at[index]) for index, pair in enumerate(pairs)]
    for move in moves:
        move.start()
    moves[0].wait()
    moves[1].wait()
    shape, rate = bs_s[...], br_s[...]
    genes = shape.shape[0]
    gene_ref[:genes] = jnp.exp(digamma_series(shape) - jnp.log(rate)).astype(BF16)
    beta = jnp.sum(shape / rate, axis=0, keepdims=True)
    moves[2].wait()
    moves[3].wait()
    shape, rate = ts_s[...], tr_s[...]
    weight = jnp.exp(digamma_series(shape) - jnp.log(rate)).astype(BF16)
    for copy in range(cell_ref.shape[0]):
        cell_ref[copy] = weight
    gene_ref[genes:] = split_rows(beta, jnp.sum(shape / rate, axis=0, keepdims=True))


def weights_call(theta_shape, theta_rate, beta_shape, beta_rate):
    cells, width = theta_shape.shape
    genes = beta_shape.shape[0]
    return pl.pallas_call(
        weights_kernel,
        in_specs=[HBM] * 4,
        out_specs=[VMEM] * 2,
        out_shape=[
            jax.ShapeDtypeStruct((8, cells, width), BF16),
            jax.ShapeDtypeStruct((genes + EXTRA, width), BF16),
        ],
        scratch_shapes=[pltpu.VMEM((cells, width), F32)] * 2
        + [pltpu.VMEM((genes, width), F32)] * 2
        + [pltpu.SemaphoreType.DMA((4,))],
        compiler_params=pltpu.CompilerParams(vmem_limit_bytes=55152 * 1024),
    )(theta_shape, theta_rate, beta_shape, beta_rate)


def main_kernel(
    ids_ref, live_ref, cell_ref, own_ref, oth_ref, counts_ref,
    cell_out, keep_out, send_out,
    ids_s, live_s, counts_s, rows_s, cols_s, acc_s, gene_s, sems, id_sem, live_sem,
):
    parts, part, width = cell_ref.shape
    block = own_ref.shape[1] - EXTRA
    sides = own_ref.shape[0]
    cells = parts * part
    groups = counts_ref.shape[0] // GROUP
    my_y, my_x, my_core = lax.axis_index("y"), lax.axis_index("x"), lax.axis_index("core")

    def fetch(group):
        here = pl.ds(group * GROUP, GROUP)
        return pltpu.make_async_copy(counts_ref.at[here], counts_s.at[here], sems.at[group])

    live_copy = pltpu.make_async_copy(live_ref, live_s, live_sem)
    ids_copy = pltpu.make_async_copy(ids_ref, ids_s, id_sem)
    live_copy.start()
    ids_copy.start()
    fetch(0).start()
    for index in range(parts):
        rows = cell_ref[index]
        rows_s[pl.ds(index * part, part), :] = rows
        cols_s[:, pl.ds(index * part, part)] = rows.T
    gene_s[...] = jnp.zeros_like(gene_s)
    live_copy.wait()
    ids_copy.wait()
    live = live_s[0, 0]
    for group in range(1, groups):
        @pl.when(GROUP * group < live)
        def _():
            fetch(group).start()

    def place(slot):
        index = ids_s[0, 0, slot]
        core, x, y = index % 2, (index // 2) % 4, index // 8
        from_x, from_y = (my_x - x + 4) % 4, (my_y - y + 4) % 4
        spot = jnp.where(core == 0, from_y * 4 + from_x, from_x * 4 + from_y)
        return index, core == my_core, spot

    def block_of(slot):
        _, mine, spot = place(slot)
        return jnp.where(mine, own_ref[spot, :block], oth_ref[spot, :block])

    for group in range(groups):
        @pl.when(GROUP * group < live)
        def _():
            slots = [GROUP * group + index for index in range(GROUP)]
            alive = [slot < live for slot in slots]
            pair = jnp.concatenate([block_of(slot) for slot in slots], axis=0)
            fetch(group).wait()
            total = jnp.zeros((width, GROUP * block), F32)
            for start in range(0, cells, CHUNK):
                here = pl.ds(start, CHUNK)
                rate = lax.dot_general(
                    rows_s[here, :], pair, (((1,), (1,)), ((), ())), preferred_element_type=F32
                )
                ratios = []
                for index in range(GROUP):
                    columns = slice(index * block, (index + 1) * block)
                    ratio = counts_s[slots[index], here, :].astype(F32) / rate[:, columns]
                    if slots[index] > 1:
                        ratio = jnp.where(alive[index], ratio, 0.0)
                    ratios.append(ratio.astype(BF16))
                ratio = jnp.concatenate(ratios, axis=1)
                term = jnp.dot(ratio, pair, preferred_element_type=F32)
                if group == 0:
                    acc_s[here, :] = term
                else:
                    acc_s[here, :] += term
                total += jnp.dot(cols_s[:, here], ratio, preferred_element_type=F32)
            total = total.T
            for k in range(GROUP):
                @pl.when(alive[k])
                def _():
                    index, mine, _ = place(slots[k])
                    gene_s[jnp.where(mine, 0, 1), index // 2] = total[k * block : (k + 1) * block]

    totals = row_totals(jnp.concatenate([own_ref[:, block:], oth_ref[:, block:]], axis=0))
    extra = split_rows(*totals)
    for index in range(parts):
        cell_out[index, :part] = acc_s[pl.ds(index * part, part), :].astype(BF16)
        cell_out[index, part:] = extra
    for index in range(sides):
        keep_out[index] = gene_s[0, index]
        send_out[index] = gene_s[1, index].astype(BF16)


def main_call(ids, live, cell_rows, own, other, counts):
    slots, cells, block = counts.shape
    parts, part, width = cell_rows.shape
    sides = own.shape[0]
    return pl.pallas_call(
        main_kernel,
        in_specs=[HBM, HBM, VMEM, VMEM, VMEM, HBM],
        out_specs=[VMEM, VMEM, VMEM],
        scratch_shapes=[
            pltpu.SMEM(ids.shape, jnp.int32),
            pltpu.SMEM(live.shape, jnp.int32),
            pltpu.VMEM((slots, cells, block), BF16),
            pltpu.VMEM((cells, width), BF16),
            pltpu.VMEM((width, cells), BF16),
            pltpu.VMEM((cells, width), F32),
            pltpu.VMEM((2, sides, block, width), F32),
            pltpu.SemaphoreType.DMA((slots // GROUP,)),
            pltpu.SemaphoreType.DMA,
            pltpu.SemaphoreType.DMA,
        ],
        out_shape=[
            jax.ShapeDtypeStruct((parts, part + EXTRA, width), BF16),
            jax.ShapeDtypeStruct((sides, block, width), F32),
            jax.ShapeDtypeStruct((sides, block, width), BF16),
        ],
        compiler_params=params(48),
    )(ids, live, cell_rows, own, other, counts)


def first_and_second():
    my_y, my_x, core = lax.axis_index("y"), lax.axis_index("x"), lax.axis_index("core")
    return core, jnp.where(core == 0, my_x, my_y), jnp.where(core == 0, my_y, my_x)


def core_sum_kernel(keep_ref, got_ref, mine_ref, *send_refs):
    core, first, _ = first_and_second()
    for row in range(4):
        for step in range(4):
            along = (first + step) % 4
            spot = jnp.where(core == 0, row * 4 + along, along * 4 + row)
            value = keep_ref[spot] + got_ref[spot].astype(F32)
            if step == 0:
                mine_ref[row] = value
            else:
                send_refs[step - 1][row] = value.astype(BF16)


def first_sum_kernel(keep_ref, a_ref, b_ref, c_ref, mine_ref, *send_refs):
    _, _, second = first_and_second()
    for step in range(4):
        spot = (second + step) % 4
        value = keep_ref[spot] + a_ref[spot].astype(F32)
        value += b_ref[spot].astype(F32) + c_ref[spot].astype(F32)
        if step == 0:
            mine_ref[...] = value
        else:
            send_refs[step - 1][...] = value.astype(BF16)


def finish(weight, stat, activity, total, shape_ref, rate_ref):
    rows, width = stat.shape
    shape_ref[...] = jnp.log(0.3 + weight.astype(F32) * stat)
    for start in range(0, rows, 128):
        here = pl.ds(start, 128)
        column = jnp.broadcast_to(activity[:, start : start + 128], (width, 128)).T
        rate_ref[here, :] = jnp.log(column + total)


def gene_finish_kernel(keep_ref, a_ref, b_ref, c_ref, got_ref, weight_ref, act_ref, shape_ref, rate_ref):
    value = keep_ref[...] + a_ref[...].astype(F32)
    value += b_ref[...].astype(F32) + c_ref[...].astype(F32)
    rows = value.shape[0]
    _, theta = row_totals(got_ref[:, got_ref.shape[1] - EXTRA :])
    finish(weight_ref[:rows], value, act_ref[...], theta, shape_ref, rate_ref)


def cell_finish_kernel(got_ref, weights_ref, act_ref, shape_ref, rate_ref):
    parts, rows, _ = weights_ref.shape
    value = got_ref[0, :rows].astype(F32)
    for index in range(1, parts):
        value += got_ref[index, :rows].astype(F32)
    beta, _ = row_totals(got_ref[:, rows:])
    finish(weights_ref[lax.axis_index("z")], value, act_ref[...], beta, shape_ref, rate_ref)


def simple_call(kernel, out_shape, *args, mib=16):
    return pl.pallas_call(
        kernel,
        in_specs=[VMEM] * len(args),
        out_specs=[VMEM] * len(out_shape),
        out_shape=out_shape,
        compiler_params=params(mib),
    )(*args)


def shift(stage, step, value):
    pairs = []
    for y in range(4):
        for x in range(4):
            for core in range(2):
                if core == stage:
                    to_y, to_x = y, (x + step) % 4
                else:
                    to_y, to_x = (y + step) % 4, x
                pairs.append(((y * 4 + x) * 2 + core, (to_y * 4 + to_x) * 2 + core))
    return lax.ppermute(value, ("y", "x", "core"), pairs)


def swap_cores(value):
    return lax.ppermute(value, "core", [(0, 1), (1, 0)])


def on_device(
    theta_shape,
    theta_rate,
    cell_activity,
    beta_shape,
    beta_rate,
    gene_activity,
    block_ids,
    live_blocks,
    counts,
):
    cells, width = theta_shape.shape
    genes = beta_shape.shape[0]
    struct = jax.ShapeDtypeStruct
    steps = (1, 2, 3)
    cell_pay, gene_pay = weights_call(theta_shape, theta_rate, beta_shape, beta_rate)
    cell_rows = lax.all_to_all(cell_pay, "z", 0, 0)
    got = {step: shift(0, step, gene_pay) for step in steps}
    line = jnp.stack([gene_pay, got[1], got[2], got[3]])
    got = {step: shift(1, step, line) for step in steps}
    ids = jnp.maximum(block_ids, 0)
    got, ids = lax.optimization_barrier((got, ids))
    own = jnp.concatenate([line, got[1], got[2], got[3]])
    other = swap_cores(own)

    cell_part, keep, send = main_call(ids, live_blocks, cell_rows, own, other, counts[0])
    cell_got = lax.all_to_all(cell_part, "z", 0, 0)
    keep, *sends = simple_call(
        core_sum_kernel,
        [struct((4, genes, width), F32)] + [struct((4, genes, width), BF16)] * 3,
        keep, swap_cores(send),
    )
    gots = [shift(0, step, sends[step - 1]) for step in steps]
    keep, *sends = simple_call(
        first_sum_kernel,
        [struct((genes, width), F32)] + [struct((genes, width), BF16)] * 3,
        keep, *gots,
    )
    gots = [shift(1, step, sends[step - 1]) for step in steps]
    log_theta = simple_call(
        cell_finish_kernel, [struct((cells, width), F32)] * 2,
        cell_got, cell_rows, cell_activity.reshape(1, cells),
    )
    gots, log_theta = lax.optimization_barrier((gots, log_theta))
    log_beta = simple_call(
        gene_finish_kernel, [struct((genes, width), F32)] * 2,
        keep, *gots, cell_got, gene_pay, gene_activity.reshape(1, genes),
    )
    return (*log_theta, *log_beta)


def solution(mesh):
    fine = Mesh(mesh.devices.reshape(4, 4, 2, 8), ("y", "x", "core", "z"))
    cells = ("y", "x", "core")
    every = cells + ("z",)
    in_specs = (
        P(every, None),
        P(every, None),
        P(every),
        P(every, None),
        P(every, None),
        P(every),
        P("z", cells, None),
        P("z", cells),
        P("z", None, cells, None),
    )
    out_specs = (P(every, None),) * 4
    return jax.shard_map(
        on_device, mesh=fine, in_specs=in_specs, out_specs=out_specs, check_vma=False
    )
```

profile of v0, /device:TPU:6, one launch (start us, length us, event | category | flops | bytes accessed | tf_op | source)
XLA Modules:
  0.0 65.0 jit_solution(6099837444782564538)
XLA Ops:
  0.6 0.0 copy-start
  0.6 2.1 %shard_map.120 = (bf16[8,256,128]{2,1,0:T(8,128)(2,1)}, bf16[144,128]{1,0:T(8,128)(2,1)S(1)}) custom-call(f32[256,128]{1,0:T(8,128)} %ts_hbm.1, f32[256,128]{1,0:T(8,128)} %tr_hbm.1, f32[128,128]{1,0:T(8,128)} %bs_hbm.1, f32[128,128]{1,0:T(8,128)} %br_hbm.1), custom_call_target="tpu_custom_call" | custom-call | tf_op jit(solution)/shard_map/pallas_call | solution.py:76
  2.7 0.9 %collective-permute-start.2 = (bf16[144,128]{1,0:T(8,128)(2,1)S(1)}, bf16[144,128]{1,0:T(8,128)(2,1)S(1)}, u32[]{:S(2)}, u32[]{:S(2)}) collective-permute-start(bf16[144,128]{1,0:T(8,128)(2,1)S(1)} %get-tuple-element.30.weight_ref), channel_id=1, source_target_pairs={{0,48},{8,200},{16,0},{24,216},{32,16},{40,232},{48,32},{56,248},{... | collective-permute-start | bytes 110600 | tf_op jit(solution)/shard_map/ppermute | solution.py:285
  3.6 2.8 %collective-permute-start.1 = (bf16[144,128]{1,0:T(8,128)(2,1)S(1)}, bf16[144,128]{1,0:T(8,128)(2,1)S(1)}, u32[]{:S(2)}, u32[]{:S(2)}) collective-permute-start(bf16[144,128]{1,0:T(8,128)(2,1)S(1)} %get-tuple-element.30.weight_ref), channel_id=1, source_target_pairs={{0,32},{8,136},{16,48},{24,152},{32,0},{40,168},{48,16},{56,184},{... | collective-permute-start | bytes 110600 | tf_op jit(solution)/shard_map/ppermute | solution.py:285
  6.5 0.4 collective-permute-start
  6.8 0.0 copy-start.1
  6.8 8.6 %all-to-all-start = ((bf16[8,256,128]{2,1,0:T(8,128)(2,1)}), bf16[8,256,128]{2,1,0:T(8,128)(2,1)S(1)}, u32[]{:S(2)}, u32[]{:S(2)}) async-start(bf16[8,256,128]{2,1,0:T(8,128)(2,1)} %get-tuple-element.32), calls=%async_computation | async-start | bytes 1048576 | tf_op jit(solution)/shard_map/all_to_all | solution.py:308
  15.5 0.7 %broadcast_maximum_fusion.ids_ref = s32[1,1,16]{2,1,0:T(1,128)S(1)} fusion(s32[1,1,16]{2,1,0:T(1,128)} %param.15), kind=kLoop, calls=%fused_computation.8 | loop fusion | flops 16 | bytes 128 | tf_op jit(solution)/shard_map/max | solution.py:312
  16.1 0.0 collective-permute-done.2
  16.1 0.0 collective-permute-done.1
  16.1 0.0 collective-permute-done
  16.2 3.1 %collective-permute-start.5 = (bf16[4,144,128]{2,1,0:T(8,128)(2,1)S(1)}, bf16[4,144,128]{2,1,0:T(8,128)(2,1)S(1)}, u32[]{:S(2)}, u32[]{:S(2)}) collective-permute-start(bf16[4,144,128]{2,1,0:T(8,128)(2,1)S(1)} %pad_maximum_fusion), channel_id=1, source_target_pairs={{0,192},{8,56},{16,208},{24,8},{32,224},{40,24},{48,240},{56,40},{... | collective-permute-start | bytes 442376 | tf_op jit(solution)/shard_map/ppermute | solution.py:285
  19.2 0.6 collective-permute-start.4
  19.9 1.0 %collective-permute-start.3 = (bf16[4,144,128]{2,1,0:T(8,128)(2,1)S(1)}, bf16[4,144,128]{2,1,0:T(8,128)(2,1)S(1)}, u32[]{:S(2)}, u32[]{:S(2)}) collective-permute-start(bf16[4,144,128]{2,1,0:T(8,128)(2,1)S(1)} %pad_maximum_fusion), channel_id=1, source_target_pairs={{0,64},{8,24},{16,80},{24,40},{32,96},{40,56},{48,112},{56,8},{64,... | collective-permute-start | bytes 442376 | tf_op jit(solution)/shard_map/ppermute | solution.py:285
  20.9 2.6 %collective-permute-done.5 = bf16[4,144,128]{2,1,0:T(8,128)(2,1)S(1)} collective-permute-done((bf16[4,144,128]{2,1,0:T(8,128)(2,1)S(1)}, bf16[4,144,128]{2,1,0:T(8,128)(2,1)S(1)}, u32[]{:S(2)}, u32[]{:S(2)}) %collective-permute-start.5) | collective-permute-done | bytes 147488 | tf_op jit(solution)/shard_map/ppermute | solution.py:285
  23.5 2.5 %collective-permute-done.4 = bf16[4,144,128]{2,1,0:T(8,128)(2,1)S(1)} collective-permute-done((bf16[4,144,128]{2,1,0:T(8,128)(2,1)S(1)}, bf16[4,144,128]{2,1,0:T(8,128)(2,1)S(1)}, u32[]{:S(2)}, u32[]{:S(2)}) %collective-permute-start.4) | collective-permute-done | bytes 147488 | tf_op jit(solution)/shard_map/ppermute | solution.py:285
  26.0 1.5 %collective-permute-done.3 = bf16[4,144,128]{2,1,0:T(8,128)(2,1)S(1)} collective-permute-done((bf16[4,144,128]{2,1,0:T(8,128)(2,1)S(1)}, bf16[4,144,128]{2,1,0:T(8,128)(2,1)S(1)}, u32[]{:S(2)}, u32[]{:S(2)}) %collective-permute-start.3) | collective-permute-done | bytes 147488 | tf_op jit(solution)/shard_map/ppermute | solution.py:285
  27.6 0.1 collective-permute-start.6
  28.3 1.3 %collective-permute-done.6.oth_ref = bf16[16,144,128]{2,1,0:T(8,128)(2,1)S(1)} collective-permute-done((bf16[16,144,128]{2,1,0:T(8,128)(2,1)S(1)}, bf16[16,144,128]{2,1,0:T(8,128)(2,1)S(1)}, u32[]{:S(2)}, u32[]{:S(2)}) %collective-permute-start.6) | collective-permute-done | bytes 589856 | tf_op jit(solution)/shard_map/ppermute | solution.py:289
  29.6 3.0 %all-to-all-done.cell_ref.weights_ref = bf16[8,256,128]{2,1,0:T(8,128)(2,1)S(1)} async-done(((bf16[8,256,128]{2,1,0:T(8,128)(2,1)}), bf16[8,256,128]{2,1,0:T(8,128)(2,1)S(1)}, u32[]{:S(2)}, u32[]{:S(2)}) %all-to-all-start) | async-done | bytes 524320 | tf_op jit(solution)/shard_map/all_to_all | solution.py:308
  32.7 6.2 %shard_map.121 = (bf16[8,272,128]{2,1,0:T(8,128)(2,1)}, f32[16,128,128]{2,1,0:T(8,128)S(1)}, bf16[16,128,128]{2,1,0:T(8,128)(2,1)S(1)}) custom-call(s32[1,1,16]{2,1,0:T(1,128)S(1)} %broadcast_maximum_fusion.ids_ref, s32[1,1]{1,0:T(1,128)S(6)} %copy.19.live_ref, bf16[8,256,128]{2,1,0:T(8,128)(2,1)S(1)} %all-to-all-done.cell_ref.weights_ref, ...), custom_call_target="tpu_custom_call" | custom-call | tf_op jit(solution)/shard_map/pallas_call | solution.py:184
  38.9 5.0 %all-to-all-start.1 = ((bf16[8,272,128]{2,1,0:T(8,128)(2,1)}), bf16[8,272,128]{2,1,0:T(8,128)(2,1)S(1)}, u32[]{:S(2)}, u32[]{:S(2)}) async-start(bf16[8,272,128]{2,1,0:T(8,128)(2,1)} %get-tuple-element.45), calls=%async_computation.1 | async-start | bytes 1114112 | tf_op jit(solution)/shard_map/all_to_all | solution.py:318
  44.0 0.8 %collective-permute-start.7 = (bf16[16,128,128]{2,1,0:T(8,128)(2,1)S(1)}, bf16[16,128,128]{2,1,0:T(8,128)(2,1)S(1)}, u32[]{:S(2)}, u32[]{:S(2)}) collective-permute-start(bf16[16,128,128]{2,1,0:T(8,128)(2,1)S(1)} %get-tuple-element.37), channel_id=1, source_target_pairs={{0,8},{8,0},{1,9},{9,1},{2,10},{10,2},{3,11},{11,3},{4,12},{12,4},... | collective-permute-start | bytes 1572872 | tf_op jit(solution)/shard_map/ppermute | solution.py:289
  44.7 1.5 %collective-permute-done.7.got_ref = bf16[16,128,128]{2,1,0:T(8,128)(2,1)S(1)} collective-permute-done((bf16[16,128,128]{2,1,0:T(8,128)(2,1)S(1)}, bf16[16,128,128]{2,1,0:T(8,128)(2,1)S(1)}, u32[]{:S(2)}, u32[]{:S(2)}) %collective-permute-start.7) | collective-permute-done | bytes 524320 | tf_op jit(solution)/shard_map/ppermute | solution.py:289
  46.2 0.1 shard_map.122
  46.4 0.3 collective-permute-start.8
  46.6 4.5 %collective-permute-start.9 = (bf16[4,128,128]{2,1,0:T(8,128)(2,1)S(1)}, bf16[4,128,128]{2,1,0:T(8,128)(2,1)S(1)}, u32[]{:S(2)}, u32[]{:S(2)}) collective-permute-start(bf16[4,128,128]{2,1,0:T(8,128)(2,1)S(1)} %get-tuple-element.40), channel_id=1, source_target_pairs={{0,32},{8,136},{16,48},{24,152},{32,0},{40,168},{48,16},{56,184},{... | collective-permute-start | bytes 393224 | tf_op jit(solution)/shard_map/ppermute | solution.py:285
  51.1 0.0 collective-permute-start.10
  51.1 0.9 %collective-permute-done.8.a_ref = bf16[4,128,128]{2,1,0:T(8,128)(2,1)S(1)} collective-permute-done((bf16[4,128,128]{2,1,0:T(8,128)(2,1)S(1)}, bf16[4,128,128]{2,1,0:T(8,128)(2,1)S(1)}, u32[]{:S(2)}, u32[]{:S(2)}) %collective-permute-start.8) | collective-permute-done | bytes 131104 | tf_op jit(solution)/shard_map/ppermute | solution.py:285
  52.0 2.1 %collective-permute-done.9.b_ref = bf16[4,128,128]{2,1,0:T(8,128)(2,1)S(1)} collective-permute-done((bf16[4,128,128]{2,1,0:T(8,128)(2,1)S(1)}, bf16[4,128,128]{2,1,0:T(8,128)(2,1)S(1)}, u32[]{:S(2)}, u32[]{:S(2)}) %collective-permute-start.9) | collective-permute-done | bytes 131104 | tf_op jit(solution)/shard_map/ppermute | solution.py:285
  54.0 3.2 %collective-permute-done.10.c_ref = bf16[4,128,128]{2,1,0:T(8,128)(2,1)S(1)} collective-permute-done((bf16[4,128,128]{2,1,0:T(8,128)(2,1)S(1)}, bf16[4,128,128]{2,1,0:T(8,128)(2,1)S(1)}, u32[]{:S(2)}, u32[]{:S(2)}) %collective-permute-start.10) | collective-permute-done | bytes 131104 | tf_op jit(solution)/shard_map/ppermute | solution.py:285
  57.3 0.1 shard_map.123
  57.3 1.2 %collective-permute-start.11 = (bf16[128,128]{1,0:T(8,128)(2,1)S(1)}, bf16[128,128]{1,0:T(8,128)(2,1)S(1)}, u32[]{:S(2)}, u32[]{:S(2)}) collective-permute-start(bf16[128,128]{1,0:T(8,128)(2,1)S(1)} %get-tuple-element.42), channel_id=1, source_target_pairs={{0,64},{8,24},{16,80},{24,40},{32,96},{40,56},{48,112},{56,8},{64,... | collective-permute-start | bytes 98312 | tf_op jit(solution)/shard_map/ppermute | solution.py:285
  58.6 0.7 %collective-permute-start.12 = (bf16[128,128]{1,0:T(8,128)(2,1)S(1)}, bf16[128,128]{1,0:T(8,128)(2,1)S(1)}, u32[]{:S(2)}, u32[]{:S(2)}) collective-permute-start(bf16[128,128]{1,0:T(8,128)(2,1)S(1)} %get-tuple-element.43), channel_id=1, source_target_pairs={{0,128},{8,40},{16,144},{24,56},{32,160},{40,8},{48,176},{56,24},{... | collective-permute-start | bytes 98312 | tf_op jit(solution)/shard_map/ppermute | solution.py:285
  59.3 2.0 %collective-permute-start.13 = (bf16[128,128]{1,0:T(8,128)(2,1)S(1)}, bf16[128,128]{1,0:T(8,128)(2,1)S(1)}, u32[]{:S(2)}, u32[]{:S(2)}) collective-permute-start(bf16[128,128]{1,0:T(8,128)(2,1)S(1)} %get-tuple-element.44), channel_id=1, source_target_pairs={{0,192},{8,56},{16,208},{24,8},{32,224},{40,24},{48,240},{56,40},{... | collective-permute-start | bytes 98312 | tf_op jit(solution)/shard_map/ppermute | solution.py:285
  61.4 2.0 %all-to-all-done.1.got_ref = bf16[8,272,128]{2,1,0:T(8,128)(2,1)S(1)} async-done(((bf16[8,272,128]{2,1,0:T(8,128)(2,1)}), bf16[8,272,128]{2,1,0:T(8,128)(2,1)S(1)}, u32[]{:S(2)}, u32[]{:S(2)}) %all-to-all-start.1) | async-done | bytes 557088 | tf_op jit(solution)/shard_map/all_to_all | solution.py:318
  63.4 0.0 copy-done
  63.4 0.8 %shard_map.124 = (f32[256,128]{1,0:T(8,128)}, f32[256,128]{1,0:T(8,128)}) custom-call(bf16[8,272,128]{2,1,0:T(8,128)(2,1)S(1)} %all-to-all-done.1.got_ref, bf16[8,256,128]{2,1,0:T(8,128)(2,1)S(1)} %all-to-all-done.cell_ref.weights_ref, f32[1,256]{1,0:T(1,128)S(1)} %bitcast.12), custom_call_target="tpu_custom_call" | custom-call | tf_op jit(solution)/shard_map/pallas_call | solution.py:266
  64.2 0.0 collective-permute-done.11.a_ref
  64.2 0.0 collective-permute-done.12.b_ref
  64.2 0.0 collective-permute-done.13.c_ref
  64.2 0.0 copy-done.1
  64.2 0.7 %shard_map.125 = (f32[128,128]{1,0:T(8,128)}, f32[128,128]{1,0:T(8,128)}) custom-call(f32[128,128]{1,0:T(8,128)S(1)} %get-tuple-element.50.keep_ref, bf16[128,128]{1,0:T(8,128)(2,1)S(1)} %collective-permute-done.11.a_ref, bf16[128,128]{1,0:T(8,128)(2,1)S(1)} %collective-permute-done.12.b_ref, bf16[128,128]{1,0:T(8,128)(2,1)S(1)} %collective-permute-done.13.c_ref, ...), custom_call_target="tpu_custom_call" | custom-call | tf_op jit(solution)/shard_map/pallas_call | solution.py:266
  (8 shorter events, 0.1 us)
Async XLA Ops:
  0.6 62.8 %copy-start = (f32[256]{0:T(256)S(1)}, f32[256]{0:T(256)}, u32[]{:S(2)}) copy-start(f32[256]{0:T(256)} %param.11) | copy-start | bytes 3076
  2.7 13.4 %collective-permute-start.2 = (bf16[144,128]{1,0:T(8,128)(2,1)S(1)}, bf16[144,128]{1,0:T(8,128)(2,1)S(1)}, u32[]{:S(2)}, u32[]{:S(2)}) collective-permute-start(bf16[144,128]{1,0:T(8,128)(2,1)S(1)} %get-tuple-element.30.weight_ref), channel_id=1, source_target_pairs={{0,48},{8,200},{16,0},{24,216},{32,16},{40,232},{48,32},{56,248},{... | collective-permute-start | bytes 110600 | tf_op jit(solution)/shard_map/ppermute | solution.py:285
  3.6 12.5 %collective-permute-start.1 = (bf16[144,128]{1,0:T(8,128)(2,1)S(1)}, bf16[144,128]{1,0:T(8,128)(2,1)S(1)}, u32[]{:S(2)}, u32[]{:S(2)}) collective-permute-start(bf16[144,128]{1,0:T(8,128)(2,1)S(1)} %get-tuple-element.30.weight_ref), channel_id=1, source_target_pairs={{0,32},{8,136},{16,48},{24,152},{32,0},{40,168},{48,16},{56,184},{... | collective-permute-start | bytes 110600 | tf_op jit(solution)/shard_map/ppermute | solution.py:285
  6.5 9.6 %collective-permute-start = (bf16[144,128]{1,0:T(8,128)(2,1)S(1)}, bf16[144,128]{1,0:T(8,128)(2,1)S(1)}, u32[]{:S(2)}, u32[]{:S(2)}) collective-permute-start(bf16[144,128]{1,0:T(8,128)(2,1)S(1)} %get-tuple-element.30.weight_ref), channel_id=1, source_target_pairs={{0,16},{8,72},{16,32},{24,88},{32,48},{40,104},{48,0},{56,120},{64... | collective-permute-start | bytes 110600 | tf_op jit(solution)/shard_map/ppermute | solution.py:285
  6.8 57.4 %copy-start.1 = (f32[128]{0:T(128)S(1)}, f32[128]{0:T(128)}, u32[]{:S(2)}) copy-start(f32[128]{0:T(128)} %param.14) | copy-start | bytes 1540
  6.8 25.8 %all-to-all-start = ((bf16[8,256,128]{2,1,0:T(8,128)(2,1)}), bf16[8,256,128]{2,1,0:T(8,128)(2,1)S(1)}, u32[]{:S(2)}, u32[]{:S(2)}) async-start(bf16[8,256,128]{2,1,0:T(8,128)(2,1)} %get-tuple-element.32), calls=%async_computation | async-start | bytes 1048576 | tf_op jit(solution)/shard_map/all_to_all | solution.py:308
  16.2 7.4 %collective-permute-start.5 = (bf16[4,144,128]{2,1,0:T(8,128)(2,1)S(1)}, bf16[4,144,128]{2,1,0:T(8,128)(2,1)S(1)}, u32[]{:S(2)}, u32[]{:S(2)}) collective-permute-start(bf16[4,144,128]{2,1,0:T(8,128)(2,1)S(1)} %pad_maximum_fusion), channel_id=1, source_target_pairs={{0,192},{8,56},{16,208},{24,8},{32,224},{40,24},{48,240},{56,40},{... | collective-permute-start | bytes 442376 | tf_op jit(solution)/shard_map/ppermute | solution.py:285
  19.2 6.8 %collective-permute-start.4 = (bf16[4,144,128]{2,1,0:T(8,128)(2,1)S(1)}, bf16[4,144,128]{2,1,0:T(8,128)(2,1)S(1)}, u32[]{:S(2)}, u32[]{:S(2)}) collective-permute-start(bf16[4,144,128]{2,1,0:T(8,128)(2,1)S(1)} %pad_maximum_fusion), channel_id=1, source_target_pairs={{0,128},{8,40},{16,144},{24,56},{32,160},{40,8},{48,176},{56,24},{... | collective-permute-start | bytes 442376 | tf_op jit(solution)/shard_map/ppermute | solution.py:285
  19.9 7.6 %collective-permute-start.3 = (bf16[4,144,128]{2,1,0:T(8,128)(2,1)S(1)}, bf16[4,144,128]{2,1,0:T(8,128)(2,1)S(1)}, u32[]{:S(2)}, u32[]{:S(2)}) collective-permute-start(bf16[4,144,128]{2,1,0:T(8,128)(2,1)S(1)} %pad_maximum_fusion), channel_id=1, source_target_pairs={{0,64},{8,24},{16,80},{24,40},{32,96},{40,56},{48,112},{56,8},{64,... | collective-permute-start | bytes 442376 | tf_op jit(solution)/shard_map/ppermute | solution.py:285
  27.6 2.1 %collective-permute-start.6 = (bf16[16,144,128]{2,1,0:T(8,128)(2,1)S(1)}, bf16[16,144,128]{2,1,0:T(8,128)(2,1)S(1)}, u32[]{:S(2)}, u32[]{:S(2)}) collective-permute-start(bf16[16,144,128]{2,1,0:T(8,128)(2,1)S(1)} %constant_dynamic-update-slice_fusion.own_ref), channel_id=1, source_target_pairs={{0,8},{8,0},{1,9},{9,1},{2,10},{10,2},{3,11},{11,3},{4,12},{12,4},... | collective-permute-start | bytes 1769480 | tf_op jit(solution)/shard_map/ppermute | solution.py:289
  38.9 24.5 %all-to-all-start.1 = ((bf16[8,272,128]{2,1,0:T(8,128)(2,1)}), bf16[8,272,128]{2,1,0:T(8,128)(2,1)S(1)}, u32[]{:S(2)}, u32[]{:S(2)}) async-start(bf16[8,272,128]{2,1,0:T(8,128)(2,1)} %get-tuple-element.45), calls=%async_computation.1 | async-start | bytes 1114112 | tf_op jit(solution)/shard_map/all_to_all | solution.py:318
  44.0 2.3 %collective-permute-start.7 = (bf16[16,128,128]{2,1,0:T(8,128)(2,1)S(1)}, bf16[16,128,128]{2,1,0:T(8,128)(2,1)S(1)}, u32[]{:S(2)}, u32[]{:S(2)}) collective-permute-start(bf16[16,128,128]{2,1,0:T(8,128)(2,1)S(1)} %get-tuple-element.37), channel_id=1, source_target_pairs={{0,8},{8,0},{1,9},{9,1},{2,10},{10,2},{3,11},{11,3},{4,12},{12,4},... | collective-permute-start | bytes 1572872 | tf_op jit(solution)/shard_map/ppermute | solution.py:289
  46.4 5.6 %collective-permute-start.8 = (bf16[4,128,128]{2,1,0:T(8,128)(2,1)S(1)}, bf16[4,128,128]{2,1,0:T(8,128)(2,1)S(1)}, u32[]{:S(2)}, u32[]{:S(2)}) collective-permute-start(bf16[4,128,128]{2,1,0:T(8,128)(2,1)S(1)} %get-tuple-element.39), channel_id=1, source_target_pairs={{0,16},{8,72},{16,32},{24,88},{32,48},{40,104},{48,0},{56,120},{64... | collective-permute-start | bytes 393224 | tf_op jit(solution)/shard_map/ppermute | solution.py:285
  46.6 7.4 %collective-permute-start.9 = (bf16[4,128,128]{2,1,0:T(8,128)(2,1)S(1)}, bf16[4,128,128]{2,1,0:T(8,128)(2,1)S(1)}, u32[]{:S(2)}, u32[]{:S(2)}) collective-permute-start(bf16[4,128,128]{2,1,0:T(8,128)(2,1)S(1)} %get-tuple-element.40), channel_id=1, source_target_pairs={{0,32},{8,136},{16,48},{24,152},{32,0},{40,168},{48,16},{56,184},{... | collective-permute-start | bytes 393224 | tf_op jit(solution)/shard_map/ppermute | solution.py:285
  51.1 6.2 %collective-permute-start.10 = (bf16[4,128,128]{2,1,0:T(8,128)(2,1)S(1)}, bf16[4,128,128]{2,1,0:T(8,128)(2,1)S(1)}, u32[]{:S(2)}, u32[]{:S(2)}) collective-permute-start(bf16[4,128,128]{2,1,0:T(8,128)(2,1)S(1)} %get-tuple-element.41), channel_id=1, source_target_pairs={{0,48},{8,200},{16,0},{24,216},{32,16},{40,232},{48,32},{56,248},{... | collective-permute-start | bytes 393224 | tf_op jit(solution)/shard_map/ppermute | solution.py:285
  57.3 6.9 %collective-permute-start.11 = (bf16[128,128]{1,0:T(8,128)(2,1)S(1)}, bf16[128,128]{1,0:T(8,128)(2,1)S(1)}, u32[]{:S(2)}, u32[]{:S(2)}) collective-permute-start(bf16[128,128]{1,0:T(8,128)(2,1)S(1)} %get-tuple-element.42), channel_id=1, source_target_pairs={{0,64},{8,24},{16,80},{24,40},{32,96},{40,56},{48,112},{56,8},{64,... | collective-permute-start | bytes 98312 | tf_op jit(solution)/shard_map/ppermute | solution.py:285
  58.6 5.6 %collective-permute-start.12 = (bf16[128,128]{1,0:T(8,128)(2,1)S(1)}, bf16[128,128]{1,0:T(8,128)(2,1)S(1)}, u32[]{:S(2)}, u32[]{:S(2)}) collective-permute-start(bf16[128,128]{1,0:T(8,128)(2,1)S(1)} %get-tuple-element.43), channel_id=1, source_target_pairs={{0,128},{8,40},{16,144},{24,56},{32,160},{40,8},{48,176},{56,24},{... | collective-permute-start | bytes 98312 | tf_op jit(solution)/shard_map/ppermute | solution.py:285
  59.3 4.9 %collective-permute-start.13 = (bf16[128,128]{1,0:T(8,128)(2,1)S(1)}, bf16[128,128]{1,0:T(8,128)(2,1)S(1)}, u32[]{:S(2)}, u32[]{:S(2)}) collective-permute-start(bf16[128,128]{1,0:T(8,128)(2,1)S(1)} %get-tuple-element.44), channel_id=1, source_target_pairs={{0,192},{8,56},{16,208},{24,8},{32,224},{40,24},{48,240},{56,40},{... | collective-permute-start | bytes 98312 | tf_op jit(solution)/shard_map/ppermute | solution.py:285
where the time goes:
time: 66.2 us; the launch traced here: 65 us
  starting transfers between devices  32.1 us (48%)
  waiting for transfers between devices  20.7 us (31%)
  Pallas kernels  10 us (15%)
  between operations  1.38 us (2%)
  other arithmetic  0.68 us (1%)
    ppermute x12, starting transfers between devices, shift(): return lax.ppermute(value, ('y', 'x', 'core'), pairs)  17.6 us
    ppermute x12, waiting for transfers between devices, shift(): return lax.ppermute(value, ('y', 'x', 'core'), pairs)  12.8 us
    all_to_all x1, starting transfers between devices, on_device(): cell_rows = lax.all_to_all(cell_pay, 'z', 0, 0)  8.6 us
    pallas_call x1, Pallas kernels, main_call(): pl.pallas_call(main_kernel, in_specs=[HBM, HBM, VMEM, VMEM, VMEM, HBM], o...  6.22 us
    all_to_all x1, starting transfers between devices, on_device(): cell_got = lax.all_to_all(cell_part, 'z', 0, 0)  5.04 us
    all_to_all x1, waiting for transfers between devices, on_device(): cell_rows = lax.all_to_all(cell_pay, 'z', 0, 0)  3.03 us
    ppermute x2, waiting for transfers between devices, swap_cores(): return lax.ppermute(value, 'core', [(0, 1), (1, 0)])  2.88 us
    pallas_call x1, Pallas kernels, weights_call(): pl.pallas_call(weights_kernel, in_specs=[HBM] * 4, out_specs=[VMEM] * 2,...  2.08 us
  transfers between devices with their start and end apart: 16, of which 10 were waited for; matrix products, arithmetic and copies ran while one was open for 1% of the time, Pallas kernels for 2%

commit v1 on v0

--- a/solution.py
+++ b/solution.py
@@ -111,8 +111,8 @@
     fetch(0).start()
     for index in range(parts):
         rows = cell_ref[index]
-        rows_s[pl.ds(index * part, part), :] = rows
-        cols_s[:, pl.ds(index * part, part)] = rows.T
+        rows_s[pl.ds(pl.multiple_of(spot_of(index) * part, part), part), :] = rows
+        cols_s[:, pl.ds(pl.multiple_of(spot_of(index) * part, part), part)] = rows.T
     gene_s[...] = jnp.zeros_like(gene_s)
     live_copy.wait()
     ids_copy.wait()
@@ -170,7 +170,7 @@
     totals = row_totals(jnp.concatenate([own_ref[:, block:], oth_ref[:, block:]], axis=0))
     extra = split_rows(*totals)
     for index in range(parts):
-        cell_out[index, :part] = acc_s[pl.ds(index * part, part), :].astype(BF16)
+        cell_out[index, :part] = acc_s[pl.ds(pl.multiple_of(spot_of(index) * part, part), part), :].astype(BF16)
         cell_out[index, part:] = extra
     for index in range(sides):
         keep_out[index] = gene_s[0, index]
@@ -259,7 +259,16 @@
     for index in range(1, parts):
         value += got_ref[index, :rows].astype(F32)
     beta, _ = row_totals(got_ref[:, rows:])
-    finish(weights_ref[lax.axis_index("z")], value, act_ref[...], beta, shape_ref, rate_ref)
+    finish(weights_ref[spot_of(lax.axis_index("z"))], value, act_ref[...], beta, shape_ref, rate_ref)
+
+
+def spot_of(index):
+    return jnp.where(lax.axis_index("core") == 0, index, 7 - index)
+
+
+def exchange(value):
+    groups = [list(range(8)), [8 + 7 - index for index in range(8)]]
+    return lax.all_to_all(value, ("core", "z"), 0, 0, axis_index_groups=groups)
 
 
 def simple_call(kernel, out_shape, *args, mib=16):
@@ -305,7 +314,7 @@
     struct = jax.ShapeDtypeStruct
     steps = (1, 2, 3)
     cell_pay, gene_pay = weights_call(theta_shape, theta_rate, beta_shape, beta_rate)
-    cell_rows = lax.all_to_all(cell_pay, "z", 0, 0)
+    cell_rows = exchange(cell_pay)
     got = {step: shift(0, step, gene_pay) for step in steps}
     line = jnp.stack([gene_pay, got[1], got[2], got[3]])
     got = {step: shift(1, step, line) for step in steps}
@@ -315,7 +324,7 @@
     other = swap_cores(own)
 
     cell_part, keep, send = main_call(ids, live_blocks, cell_rows, own, other, counts[0])
-    cell_got = lax.all_to_all(cell_part, "z", 0, 0)
+    cell_got = exchange(cell_part)
     keep, *sends = simple_call(
         core_sum_kernel,
         [struct((4, genes, width), F32)] + [struct((4, genes, width), BF16)] * 3,

time: 66.2 us -> 64.8 us (0.979)
  starting transfers between devices: 32.1 us -> 35.5 us
  waiting for transfers between devices: 20.7 us -> 18.1 us
  Pallas kernels: 10 us -> 8.36 us
    all_to_all x2, starting transfers between devices: 13.6 us -> 19.7 us  [exchange(): return lax.all_to_all(value, ('core', 'z'), 0, 0, axis_index_groups=groups)]
    all_to_all x2, waiting for transfers between devices: 5.06 us -> 0.51 us  [exchange(): return lax.all_to_all(value, ('core', 'z'), 0, 0, axis_index_groups=groups)]
    ppermute x12, starting transfers between devices: 17.6 us -> 15.7 us  [shift(): return lax.ppermute(value, ('y', 'x', 'core'), pairs)]
    pallas_call x1, Pallas kernels: 6.22 us -> 4.55 us  [main_call(): pl.pallas_call(main_kernel, in_specs=[HBM, HBM, VMEM, VMEM, VMEM, HBM], o...]
    ppermute x12, waiting for transfers between devices: 12.8 us -> 14.3 us  [shift(): return lax.ppermute(value, ('y', 'x', 'core'), pairs)]
    ppermute x2, starting transfers between devices: 0.85 us -> 0.1 us  [swap_cores(): return lax.ppermute(value, 'core', [(0, 1), (1, 0)])]
  transfers between devices with their start and end apart: 16 -> 16, of which waited for: 10 -> 12; matrix products, arithmetic and copies ran while one was open for 1% -> 1% of each run, Pallas kernels for 2% -> 2%
where the time goes in v1:
time: 64.8 us; the launch traced here: 64.1 us
  starting transfers between devices  35.5 us (55%)
  waiting for transfers between devices  18.1 us (28%)
  Pallas kernels  8.36 us (13%)
  between operations  1.39 us (2%)
  other arithmetic  0.68 us (1%)
    all_to_all x2, starting transfers between devices, exchange(): return lax.all_to_all(value, ('core', 'z'), 0, 0, axis_index_groups=groups)  19.7 us
    ppermute x12, starting transfers between devices, shift(): return lax.ppermute(value, ('y', 'x', 'core'), pairs)  15.7 us
    ppermute x12, waiting for transfers between devices, shift(): return lax.ppermute(value, ('y', 'x', 'core'), pairs)  14.3 us
    pallas_call x1, Pallas kernels, main_call(): pl.pallas_call(main_kernel, in_specs=[HBM, HBM, VMEM, VMEM, VMEM, HBM], o...  4.55 us
    ppermute x2, waiting for transfers between devices, swap_cores(): return lax.ppermute(value, 'core', [(0, 1), (1, 0)])  3.25 us
    pallas_call x1, Pallas kernels, weights_call(): pl.pallas_call(weights_kernel, in_specs=[HBM] * 4, out_specs=[VMEM] * 2,...  2.08 us
    pallas_call x4, Pallas kernels, simple_call(): pl.pallas_call(kernel, in_specs=[VMEM] * len(args), out_specs=[VMEM] * le...  1.74 us
  transfers between devices with their start and end apart: 16, of which 12 were waited for; matrix products, arithmetic and copies ran while one was open for 1% of the time, Pallas kernels for 2%

profile of v1, /device:TPU:6, one launch (start us, length us, event | category | flops | bytes accessed | tf_op | source)
XLA Modules:
  0.0 64.1 jit_solution(7722979967306995107)
XLA Ops:
  0.6 0.0 copy-start
  0.6 2.1 %shard_map.120 = (bf16[8,256,128]{2,1,0:T(8,128)(2,1)}, bf16[144,128]{1,0:T(8,128)(2,1)S(1)}) custom-call(f32[256,128]{1,0:T(8,128)} %ts_hbm.1, f32[256,128]{1,0:T(8,128)} %tr_hbm.1, f32[128,128]{1,0:T(8,128)} %bs_hbm.1, f32[128,128]{1,0:T(8,128)} %br_hbm.1), custom_call_target="tpu_custom_call" | custom-call | tf_op jit(solution)/shard_map/pallas_call | solution.py:76
  2.7 0.9 %collective-permute-start.2 = (bf16[144,128]{1,0:T(8,128)(2,1)S(1)}, bf16[144,128]{1,0:T(8,128)(2,1)S(1)}, u32[]{:S(2)}, u32[]{:S(2)}) collective-permute-start(bf16[144,128]{1,0:T(8,128)(2,1)S(1)} %get-tuple-element.30.weight_ref), channel_id=1, source_target_pairs={{0,48},{8,200},{16,0},{24,216},{32,16},{40,232},{48,32},{56,248},{... | collective-permute-start | bytes 110600 | tf_op jit(solution)/shard_map/ppermute | solution.py:294
  3.6 2.8 %collective-permute-start.1 = (bf16[144,128]{1,0:T(8,128)(2,1)S(1)}, bf16[144,128]{1,0:T(8,128)(2,1)S(1)}, u32[]{:S(2)}, u32[]{:S(2)}) collective-permute-start(bf16[144,128]{1,0:T(8,128)(2,1)S(1)} %get-tuple-element.30.weight_ref), channel_id=1, source_target_pairs={{0,32},{8,136},{16,48},{24,152},{32,0},{40,168},{48,16},{56,184},{... | collective-permute-start | bytes 110600 | tf_op jit(solution)/shard_map/ppermute | solution.py:294
  6.5 0.4 collective-permute-start
  6.8 0.0 copy-start.1
  6.8 8.6 %all-to-all-start = ((bf16[8,256,128]{2,1,0:T(8,128)(2,1)}), bf16[8,256,128]{2,1,0:T(8,128)(2,1)S(1)}, u32[]{:S(2)}, u32[]{:S(2)}) async-start(bf16[8,256,128]{2,1,0:T(8,128)(2,1)} %get-tuple-element.32), calls=%async_computation | async-start | bytes 1048576 | tf_op jit(solution)/shard_map/all_to_all | solution.py:271
  15.5 0.7 %broadcast_maximum_fusion.ids_ref = s32[1,1,16]{2,1,0:T(1,128)S(1)} fusion(s32[1,1,16]{2,1,0:T(1,128)} %param.15), kind=kLoop, calls=%fused_computation.8 | loop fusion | flops 16 | bytes 128 | tf_op jit(solution)/shard_map/max | solution.py:321
  16.1 0.0 collective-permute-done.2
  16.1 0.0 collective-permute-done.1
  16.1 0.0 collective-permute-done
  16.2 3.1 %collective-permute-start.5 = (bf16[4,144,128]{2,1,0:T(8,128)(2,1)S(1)}, bf16[4,144,128]{2,1,0:T(8,128)(2,1)S(1)}, u32[]{:S(2)}, u32[]{:S(2)}) collective-permute-start(bf16[4,144,128]{2,1,0:T(8,128)(2,1)S(1)} %pad_maximum_fusion), channel_id=1, source_target_pairs={{0,192},{8,56},{16,208},{24,8},{32,224},{40,24},{48,240},{56,40},{... | collective-permute-start | bytes 442376 | tf_op jit(solution)/shard_map/ppermute | solution.py:294
  19.2 0.6 collective-permute-start.4
  19.9 1.0 %collective-permute-start.3 = (bf16[4,144,128]{2,1,0:T(8,128)(2,1)S(1)}, bf16[4,144,128]{2,1,0:T(8,128)(2,1)S(1)}, u32[]{:S(2)}, u32[]{:S(2)}) collective-permute-start(bf16[4,144,128]{2,1,0:T(8,128)(2,1)S(1)} %pad_maximum_fusion), channel_id=1, source_target_pairs={{0,64},{8,24},{16,80},{24,40},{32,96},{40,56},{48,112},{56,8},{64,... | collective-permute-start | bytes 442376 | tf_op jit(solution)/shard_map/ppermute | solution.py:294
  20.9 2.6 %collective-permute-done.5 = bf16[4,144,128]{2,1,0:T(8,128)(2,1)S(1)} collective-permute-done((bf16[4,144,128]{2,1,0:T(8,128)(2,1)S(1)}, bf16[4,144,128]{2,1,0:T(8,128)(2,1)S(1)}, u32[]{:S(2)}, u32[]{:S(2)}) %collective-permute-start.5) | collective-permute-done | bytes 147488 | tf_op jit(solution)/shard_map/ppermute | solution.py:294
  23.5 2.5 %collective-permute-done.4 = bf16[4,144,128]{2,1,0:T(8,128)(2,1)S(1)} collective-permute-done((bf16[4,144,128]{2,1,0:T(8,128)(2,1)S(1)}, bf16[4,144,128]{2,1,0:T(8,128)(2,1)S(1)}, u32[]{:S(2)}, u32[]{:S(2)}) %collective-permute-start.4) | collective-permute-done | bytes 147488 | tf_op jit(solution)/shard_map/ppermute | solution.py:294
  26.0 1.5 %collective-permute-done.3 = bf16[4,144,128]{2,1,0:T(8,128)(2,1)S(1)} collective-permute-done((bf16[4,144,128]{2,1,0:T(8,128)(2,1)S(1)}, bf16[4,144,128]{2,1,0:T(8,128)(2,1)S(1)}, u32[]{:S(2)}, u32[]{:S(2)}) %collective-permute-start.3) | collective-permute-done | bytes 147488 | tf_op jit(solution)/shard_map/ppermute | solution.py:294
  27.6 0.1 collective-permute-start.6
  28.3 1.3 %collective-permute-done.6.oth_ref = bf16[16,144,128]{2,1,0:T(8,128)(2,1)S(1)} collective-permute-done((bf16[16,144,128]{2,1,0:T(8,128)(2,1)S(1)}, bf16[16,144,128]{2,1,0:T(8,128)(2,1)S(1)}, u32[]{:S(2)}, u32[]{:S(2)}) %collective-permute-start.6) | collective-permute-done | bytes 589856 | tf_op jit(solution)/shard_map/ppermute | solution.py:298
  29.6 0.5 all-to-all-done.cell_ref.weights_ref
  30.2 4.5 %shard_map.121 = (bf16[8,272,128]{2,1,0:T(8,128)(2,1)}, f32[16,128,128]{2,1,0:T(8,128)S(1)}, bf16[16,128,128]{2,1,0:T(8,128)(2,1)S(1)}) custom-call(s32[1,1,16]{2,1,0:T(1,128)S(1)} %broadcast_maximum_fusion.ids_ref, s32[1,1]{1,0:T(1,128)S(6)} %copy.19.live_ref, bf16[8,256,128]{2,1,0:T(8,128)(2,1)S(1)} %all-to-all-done.cell_ref.weights_ref, ...), custom_call_target="tpu_custom_call" | custom-call | tf_op jit(solution)/shard_map/pallas_call | solution.py:184
  34.7 11.1 %all-to-all-start.1 = ((bf16[8,272,128]{2,1,0:T(8,128)(2,1)}), bf16[8,272,128]{2,1,0:T(8,128)(2,1)S(1)}, u32[]{:S(2)}, u32[]{:S(2)}) async-start(bf16[8,272,128]{2,1,0:T(8,128)(2,1)} %get-tuple-element.45), calls=%async_computation.1 | async-start | bytes 1114112 | tf_op jit(solution)/shard_map/all_to_all | solution.py:271
  45.8 0.0 collective-permute-start.7
  45.8 1.9 %collective-permute-done.7.got_ref = bf16[16,128,128]{2,1,0:T(8,128)(2,1)S(1)} collective-permute-done((bf16[16,128,128]{2,1,0:T(8,128)(2,1)S(1)}, bf16[16,128,128]{2,1,0:T(8,128)(2,1)S(1)}, u32[]{:S(2)}, u32[]{:S(2)}) %collective-permute-start.7) | collective-permute-done | bytes 524320 | tf_op jit(solution)/shard_map/ppermute | solution.py:298
  47.7 0.1 shard_map.122
  47.8 0.7 %collective-permute-start.8 = (bf16[4,128,128]{2,1,0:T(8,128)(2,1)S(1)}, bf16[4,128,128]{2,1,0:T(8,128)(2,1)S(1)}, u32[]{:S(2)}, u32[]{:S(2)}) collective-permute-start(bf16[4,128,128]{2,1,0:T(8,128)(2,1)S(1)} %get-tuple-element.39), channel_id=1, source_target_pairs={{0,16},{8,72},{16,32},{24,88},{32,48},{40,104},{48,0},{56,120},{64... | collective-permute-start | bytes 393224 | tf_op jit(solution)/shard_map/ppermute | solution.py:294
  48.5 2.1 %collective-permute-start.9 = (bf16[4,128,128]{2,1,0:T(8,128)(2,1)S(1)}, bf16[4,128,128]{2,1,0:T(8,128)(2,1)S(1)}, u32[]{:S(2)}, u32[]{:S(2)}) collective-permute-start(bf16[4,128,128]{2,1,0:T(8,128)(2,1)S(1)} %get-tuple-element.40), channel_id=1, source_target_pairs={{0,32},{8,136},{16,48},{24,152},{32,0},{40,168},{48,16},{56,184},{... | collective-permute-start | bytes 393224 | tf_op jit(solution)/shard_map/ppermute | solution.py:294
  50.7 0.0 collective-permute-start.10
  50.7 2.2 %collective-permute-done.8.a_ref = bf16[4,128,128]{2,1,0:T(8,128)(2,1)S(1)} collective-permute-done((bf16[4,128,128]{2,1,0:T(8,128)(2,1)S(1)}, bf16[4,128,128]{2,1,0:T(8,128)(2,1)S(1)}, u32[]{:S(2)}, u32[]{:S(2)}) %collective-permute-start.8) | collective-permute-done | bytes 131104 | tf_op jit(solution)/shard_map/ppermute | solution.py:294
  52.9 2.1 %collective-permute-done.9.b_ref = bf16[4,128,128]{2,1,0:T(8,128)(2,1)S(1)} collective-permute-done((bf16[4,128,128]{2,1,0:T(8,128)(2,1)S(1)}, bf16[4,128,128]{2,1,0:T(8,128)(2,1)S(1)}, u32[]{:S(2)}, u32[]{:S(2)}) %collective-permute-start.9) | collective-permute-done | bytes 131104 | tf_op jit(solution)/shard_map/ppermute | solution.py:294
  55.0 1.9 %collective-permute-done.10.c_ref = bf16[4,128,128]{2,1,0:T(8,128)(2,1)S(1)} collective-permute-done((bf16[4,128,128]{2,1,0:T(8,128)(2,1)S(1)}, bf16[4,128,128]{2,1,0:T(8,128)(2,1)S(1)}, u32[]{:S(2)}, u32[]{:S(2)}) %collective-permute-start.10) | collective-permute-done | bytes 131104 | tf_op jit(solution)/shard_map/ppermute | solution.py:294
  56.9 0.1 shard_map.123
  56.9 0.1 collective-permute-start.11
  57.0 2.3 %collective-permute-start.12 = (bf16[128,128]{1,0:T(8,128)(2,1)S(1)}, bf16[128,128]{1,0:T(8,128)(2,1)S(1)}, u32[]{:S(2)}, u32[]{:S(2)}) collective-permute-start(bf16[128,128]{1,0:T(8,128)(2,1)S(1)} %get-tuple-element.43), channel_id=1, source_target_pairs={{0,128},{8,40},{16,144},{24,56},{32,160},{40,8},{48,176},{56,24},{... | collective-permute-start | bytes 98312 | tf_op jit(solution)/shard_map/ppermute | solution.py:294
  59.4 1.6 %collective-permute-start.13 = (bf16[128,128]{1,0:T(8,128)(2,1)S(1)}, bf16[128,128]{1,0:T(8,128)(2,1)S(1)}, u32[]{:S(2)}, u32[]{:S(2)}) collective-permute-start(bf16[128,128]{1,0:T(8,128)(2,1)S(1)} %get-tuple-element.44), channel_id=1, source_target_pairs={{0,192},{8,56},{16,208},{24,8},{32,224},{40,24},{48,240},{56,40},{... | collective-permute-start | bytes 98312 | tf_op jit(solution)/shard_map/ppermute | solution.py:294
  61.0 0.0 all-to-all-done.1.got_ref
  61.0 0.0 copy-done
  61.0 0.8 %shard_map.124 = (f32[256,128]{1,0:T(8,128)}, f32[256,128]{1,0:T(8,128)}) custom-call(bf16[8,272,128]{2,1,0:T(8,128)(2,1)S(1)} %all-to-all-done.1.got_ref, bf16[8,256,128]{2,1,0:T(8,128)(2,1)S(1)} %all-to-all-done.cell_ref.weights_ref, f32[1,256]{1,0:T(1,128)S(1)} %bitcast.12), custom_call_target="tpu_custom_call" | custom-call | tf_op jit(solution)/shard_map/pallas_call | solution.py:275
  61.8 0.3 collective-permute-done.11.a_ref
  62.1 0.4 collective-permute-done.12.b_ref
  62.5 0.8 %collective-permute-done.13.c_ref = bf16[128,128]{1,0:T(8,128)(2,1)S(1)} collective-permute-done((bf16[128,128]{1,0:T(8,128)(2,1)S(1)}, bf16[128,128]{1,0:T(8,128)(2,1)S(1)}, u32[]{:S(2)}, u32[]{:S(2)}) %collective-permute-start.13) | collective-permute-done | bytes 32800 | tf_op jit(solution)/shard_map/ppermute | solution.py:294
  63.3 0.0 copy-done.1
  63.3 0.7 %shard_map.125 = (f32[128,128]{1,0:T(8,128)}, f32[128,128]{1,0:T(8,128)}) custom-call(f32[128,128]{1,0:T(8,128)S(1)} %get-tuple-element.50.keep_ref, bf16[128,128]{1,0:T(8,128)(2,1)S(1)} %collective-permute-done.11.a_ref, bf16[128,128]{1,0:T(8,128)(2,1)S(1)} %collective-permute-done.12.b_ref, bf16[128,128]{1,0:T(8,128)(2,1)S(1)} %collective-permute-done.13.c_ref, ...), custom_call_target="tpu_custom_call" | custom-call | tf_op jit(solution)/shard_map/pallas_call | solution.py:275
  (8 shorter events, 0.1 us)
Async XLA Ops:
  0.6 60.3 %copy-start = (f32[256]{0:T(256)S(1)}, f32[256]{0:T(256)}, u32[]{:S(2)}) copy-start(f32[256]{0:T(256)} %param.11) | copy-start | bytes 3076
  2.7 13.4 %collective-permute-start.2 = (bf16[144,128]{1,0:T(8,128)(2,1)S(1)}, bf16[144,128]{1,0:T(8,128)(2,1)S(1)}, u32[]{:S(2)}, u32[]{:S(2)}) collective-permute-start(bf16[144,128]{1,0:T(8,128)(2,1)S(1)} %get-tuple-element.30.weight_ref), channel_id=1, source_target_pairs={{0,48},{8,200},{16,0},{24,216},{32,16},{40,232},{48,32},{56,248},{... | collective-permute-start | bytes 110600 | tf_op jit(solution)/shard_map/ppermute | solution.py:294
  3.6 12.5 %collective-permute-start.1 = (bf16[144,128]{1,0:T(8,128)(2,1)S(1)}, bf16[144,128]{1,0:T(8,128)(2,1)S(1)}, u32[]{:S(2)}, u32[]{:S(2)}) collective-permute-start(bf16[144,128]{1,0:T(8,128)(2,1)S(1)} %get-tuple-element.30.weight_ref), channel_id=1, source_target_pairs={{0,32},{8,136},{16,48},{24,152},{32,0},{40,168},{48,16},{56,184},{... | collective-permute-start | bytes 110600 | tf_op jit(solution)/shard_map/ppermute | solution.py:294
  6.5 9.6 %collective-permute-start = (bf16[144,128]{1,0:T(8,128)(2,1)S(1)}, bf16[144,128]{1,0:T(8,128)(2,1)S(1)}, u32[]{:S(2)}, u32[]{:S(2)}) collective-permute-start(bf16[144,128]{1,0:T(8,128)(2,1)S(1)} %get-tuple-element.30.weight_ref), channel_id=1, source_target_pairs={{0,16},{8,72},{16,32},{24,88},{32,48},{40,104},{48,0},{56,120},{64... | collective-permute-start | bytes 110600 | tf_op jit(solution)/shard_map/ppermute | solution.py:294
  6.8 56.5 %copy-start.1 = (f32[128]{0:T(128)S(1)}, f32[128]{0:T(128)}, u32[]{:S(2)}) copy-start(f32[128]{0:T(128)} %param.14) | copy-start | bytes 1540
  6.8 23.3 %all-to-all-start = ((bf16[8,256,128]{2,1,0:T(8,128)(2,1)}), bf16[8,256,128]{2,1,0:T(8,128)(2,1)S(1)}, u32[]{:S(2)}, u32[]{:S(2)}) async-start(bf16[8,256,128]{2,1,0:T(8,128)(2,1)} %get-tuple-element.32), calls=%async_computation | async-start | bytes 1048576 | tf_op jit(solution)/shard_map/all_to_all | solution.py:271
  16.2 7.4 %collective-permute-start.5 = (bf16[4,144,128]{2,1,0:T(8,128)(2,1)S(1)}, bf16[4,144,128]{2,1,0:T(8,128)(2,1)S(1)}, u32[]{:S(2)}, u32[]{:S(2)}) collective-permute-start(bf16[4,144,128]{2,1,0:T(8,128)(2,1)S(1)} %pad_maximum_fusion), channel_id=1, source_target_pairs={{0,192},{8,56},{16,208},{24,8},{32,224},{40,24},{48,240},{56,40},{... | collective-permute-start | bytes 442376 | tf_op jit(solution)/shard_map/ppermute | solution.py:294
  19.2 6.8 %collective-permute-start.4 = (bf16[4,144,128]{2,1,0:T(8,128)(2,1)S(1)}, bf16[4,144,128]{2,1,0:T(8,128)(2,1)S(1)}, u32[]{:S(2)}, u32[]{:S(2)}) collective-permute-start(bf16[4,144,128]{2,1,0:T(8,128)(2,1)S(1)} %pad_maximum_fusion), channel_id=1, source_target_pairs={{0,128},{8,40},{16,144},{24,56},{32,160},{40,8},{48,176},{56,24},{... | collective-permute-start | bytes 442376 | tf_op jit(solution)/shard_map/ppermute | solution.py:294
  19.9 7.6 %collective-permute-start.3 = (bf16[4,144,128]{2,1,0:T(8,128)(2,1)S(1)}, bf16[4,144,128]{2,1,0:T(8,128)(2,1)S(1)}, u32[]{:S(2)}, u32[]{:S(2)}) collective-permute-start(bf16[4,144,128]{2,1,0:T(8,128)(2,1)S(1)} %pad_maximum_fusion), channel_id=1, source_target_pairs={{0,64},{8,24},{16,80},{24,40},{32,96},{40,56},{48,112},{56,8},{64,... | collective-permute-start | bytes 442376 | tf_op jit(solution)/shard_map/ppermute | solution.py:294
  27.6 2.1 %collective-permute-start.6 = (bf16[16,144,128]{2,1,0:T(8,128)(2,1)S(1)}, bf16[16,144,128]{2,1,0:T(8,128)(2,1)S(1)}, u32[]{:S(2)}, u32[]{:S(2)}) collective-permute-start(bf16[16,144,128]{2,1,0:T(8,128)(2,1)S(1)} %constant_dynamic-update-slice_fusion.own_ref), channel_id=1, source_target_pairs={{0,8},{8,0},{1,9},{9,1},{2,10},{10,2},{3,11},{11,3},{4,12},{12,4},... | collective-permute-start | bytes 1769480 | tf_op jit(solution)/shard_map/ppermute | solution.py:298
  34.7 26.3 %all-to-all-start.1 = ((bf16[8,272,128]{2,1,0:T(8,128)(2,1)}), bf16[8,272,128]{2,1,0:T(8,128)(2,1)S(1)}, u32[]{:S(2)}, u32[]{:S(2)}) async-start(bf16[8,272,128]{2,1,0:T(8,128)(2,1)} %get-tuple-element.45), calls=%async_computation.1 | async-start | bytes 1114112 | tf_op jit(solution)/shard_map/all_to_all | solution.py:271
  45.8 1.9 %collective-permute-start.7 = (bf16[16,128,128]{2,1,0:T(8,128)(2,1)S(1)}, bf16[16,128,128]{2,1,0:T(8,128)(2,1)S(1)}, u32[]{:S(2)}, u32[]{:S(2)}) collective-permute-start(bf16[16,128,128]{2,1,0:T(8,128)(2,1)S(1)} %get-tuple-element.37), channel_id=1, source_target_pairs={{0,8},{8,0},{1,9},{9,1},{2,10},{10,2},{3,11},{11,3},{4,12},{12,4},... | collective-permute-start | bytes 1572872 | tf_op jit(solution)/shard_map/ppermute | solution.py:298
  47.8 5.0 %collective-permute-start.8 = (bf16[4,128,128]{2,1,0:T(8,128)(2,1)S(1)}, bf16[4,128,128]{2,1,0:T(8,128)(2,1)S(1)}, u32[]{:S(2)}, u32[]{:S(2)}) collective-permute-start(bf16[4,128,128]{2,1,0:T(8,128)(2,1)S(1)} %get-tuple-element.39), channel_id=1, source_target_pairs={{0,16},{8,72},{16,32},{24,88},{32,48},{40,104},{48,0},{56,120},{64... | collective-permute-start | bytes 393224 | tf_op jit(solution)/shard_map/ppermute | solution.py:294
  48.5 6.5 %collective-permute-start.9 = (bf16[4,128,128]{2,1,0:T(8,128)(2,1)S(1)}, bf16[4,128,128]{2,1,0:T(8,128)(2,1)S(1)}, u32[]{:S(2)}, u32[]{:S(2)}) collective-permute-start(bf16[4,128,128]{2,1,0:T(8,128)(2,1)S(1)} %get-tuple-element.40), channel_id=1, source_target_pairs={{0,32},{8,136},{16,48},{24,152},{32,0},{40,168},{48,16},{56,184},{... | collective-permute-start | bytes 393224 | tf_op jit(solution)/shard_map/ppermute | solution.py:294
  50.7 6.2 %collective-permute-start.10 = (bf16[4,128,128]{2,1,0:T(8,128)(2,1)S(1)}, bf16[4,128,128]{2,1,0:T(8,128)(2,1)S(1)}, u32[]{:S(2)}, u32[]{:S(2)}) collective-permute-start(bf16[4,128,128]{2,1,0:T(8,128)(2,1)S(1)} %get-tuple-element.41), channel_id=1, source_target_pairs={{0,48},{8,200},{16,0},{24,216},{32,16},{40,232},{48,32},{56,248},{... | collective-permute-start | bytes 393224 | tf_op jit(solution)/shard_map/ppermute | solution.py:294
  56.9 5.2 %collective-permute-start.11 = (bf16[128,128]{1,0:T(8,128)(2,1)S(1)}, bf16[128,128]{1,0:T(8,128)(2,1)S(1)}, u32[]{:S(2)}, u32[]{:S(2)}) collective-permute-start(bf16[128,128]{1,0:T(8,128)(2,1)S(1)} %get-tuple-element.42), channel_id=1, source_target_pairs={{0,64},{8,24},{16,80},{24,40},{32,96},{40,56},{48,112},{56,8},{64,... | collective-permute-start | bytes 98312 | tf_op jit(solution)/shard_map/ppermute | solution.py:294
  57.0 5.5 %collective-permute-start.12 = (bf16[128,128]{1,0:T(8,128)(2,1)S(1)}, bf16[128,128]{1,0:T(8,128)(2,1)S(1)}, u32[]{:S(2)}, u32[]{:S(2)}) collective-permute-start(bf16[128,128]{1,0:T(8,128)(2,1)S(1)} %get-tuple-element.43), channel_id=1, source_target_pairs={{0,128},{8,40},{16,144},{24,56},{32,160},{40,8},{48,176},{56,24},{... | collective-permute-start | bytes 98312 | tf_op jit(solution)/shard_map/ppermute | solution.py:294
  59.4 4.0 %collective-permute-start.13 = (bf16[128,128]{1,0:T(8,128)(2,1)S(1)}, bf16[128,128]{1,0:T(8,128)(2,1)S(1)}, u32[]{:S(2)}, u32[]{:S(2)}) collective-permute-start(bf16[128,128]{1,0:T(8,128)(2,1)S(1)} %get-tuple-element.44), channel_id=1, source_target_pairs={{0,192},{8,56},{16,208},{24,8},{32,224},{40,24},{48,240},{56,40},{... | collective-permute-start | bytes 98312 | tf_op jit(solution)/shard_map/ppermute | solution.py:294

commit v2 on v1

--- a/solution.py
+++ b/solution.py
@@ -318,8 +318,8 @@
     got = {step: shift(0, step, gene_pay) for step in steps}
     line = jnp.stack([gene_pay, got[1], got[2], got[3]])
     got = {step: shift(1, step, line) for step in steps}
-    ids = jnp.maximum(block_ids, 0)
-    got, ids = lax.optimization_barrier((got, ids))
+    got[1], ids = lax.optimization_barrier((got[1], block_ids))
+    ids = jnp.maximum(ids, 0)
     own = jnp.concatenate([line, got[1], got[2], got[3]])
     other = swap_cores(own)
 

time: 64.8 us -> 65 us (level)
    all_to_all x2, waiting for transfers between devices: 0.51 us -> 1.55 us  [exchange(): return lax.all_to_all(value, ('core', 'z'), 0, 0, axis_index_groups=groups)]
    ppermute x2, waiting for transfers between devices: 3.25 us -> 2.45 us  [swap_cores(): return lax.ppermute(value, 'core', [(0, 1), (1, 0)])]
    ppermute x12, starting transfers between devices: 15.7 us -> 15 us  [shift(): return lax.ppermute(value, ('y', 'x', 'core'), pairs)]
  transfers between devices with their start and end apart: 16 -> 16, of which waited for: 12 -> 9; matrix products, arithmetic and copies ran while one was open for 1% -> 1% of each run, Pallas kernels for 2% -> 2%
where the time goes in v2:
time: 65 us; the launch traced here: 64.2 us
  starting transfers between devices  35.2 us (54%)
  waiting for transfers between devices  18.5 us (28%)
  Pallas kernels  8.33 us (13%)
  between operations  1.41 us (2%)
  other arithmetic  0.68 us (1%)
    all_to_all x2, starting transfers between devices, exchange(): return lax.all_to_all(value, ('core', 'z'), 0, 0, axis_index_groups=groups)  20 us
    ppermute x12, starting transfers between devices, shift(): return lax.ppermute(value, ('y', 'x', 'core'), pairs)  15 us
    ppermute x12, waiting for transfers between devices, shift(): return lax.ppermute(value, ('y', 'x', 'core'), pairs)  14.5 us
    pallas_call x1, Pallas kernels, main_call(): pl.pallas_call(main_kernel, in_specs=[HBM, HBM, VMEM, VMEM, VMEM, HBM], o...  4.54 us
    ppermute x2, waiting for transfers between devices, swap_cores(): return lax.ppermute(value, 'core', [(0, 1), (1, 0)])  2.45 us
    pallas_call x1, Pallas kernels, weights_call(): pl.pallas_call(weights_kernel, in_specs=[HBM] * 4, out_specs=[VMEM] * 2,...  2.08 us
    pallas_call x4, Pallas kernels, simple_call(): pl.pallas_call(kernel, in_specs=[VMEM] * len(args), out_specs=[VMEM] * le...  1.71 us
    all_to_all x2, waiting for transfers between devices, exchange(): return lax.all_to_all(value, ('core', 'z'), 0, 0, axis_index_groups=groups)  1.55 us
  transfers between devices with their start and end apart: 16, of which 9 were waited for; matrix products, arithmetic and copies ran while one was open for 1% of the time, Pallas kernels for 2%

profile of v2, /device:TPU:6, one launch (start us, length us, event | category | flops | bytes accessed | tf_op | source)
XLA Modules:
  0.0 64.2 jit_solution(1339660502319646707)
XLA Ops:
  0.6 0.0 copy-start
  0.6 2.1 %shard_map.120 = (bf16[8,256,128]{2,1,0:T(8,128)(2,1)}, bf16[144,128]{1,0:T(8,128)(2,1)S(1)}) custom-call(f32[256,128]{1,0:T(8,128)} %ts_hbm.1, f32[256,128]{1,0:T(8,128)} %tr_hbm.1, f32[128,128]{1,0:T(8,128)} %bs_hbm.1, f32[128,128]{1,0:T(8,128)} %br_hbm.1), custom_call_target="tpu_custom_call" | custom-call | tf_op jit(solution)/shard_map/pallas_call | solution.py:76
  2.7 0.9 %collective-permute-start.2 = (bf16[144,128]{1,0:T(8,128)(2,1)S(1)}, bf16[144,128]{1,0:T(8,128)(2,1)S(1)}, u32[]{:S(2)}, u32[]{:S(2)}) collective-permute-start(bf16[144,128]{1,0:T(8,128)(2,1)S(1)} %get-tuple-element.28.weight_ref), channel_id=1, source_target_pairs={{0,48},{8,200},{16,0},{24,216},{32,16},{40,232},{48,32},{56,248},{... | collective-permute-start | bytes 110600 | tf_op jit(solution)/shard_map/ppermute | solution.py:294
  3.6 2.8 %collective-permute-start.1 = (bf16[144,128]{1,0:T(8,128)(2,1)S(1)}, bf16[144,128]{1,0:T(8,128)(2,1)S(1)}, u32[]{:S(2)}, u32[]{:S(2)}) collective-permute-start(bf16[144,128]{1,0:T(8,128)(2,1)S(1)} %get-tuple-element.28.weight_ref), channel_id=1, source_target_pairs={{0,32},{8,136},{16,48},{24,152},{32,0},{40,168},{48,16},{56,184},{... | collective-permute-start | bytes 110600 | tf_op jit(solution)/shard_map/ppermute | solution.py:294
  6.5 0.4 collective-permute-start
  6.8 0.0 copy-start.1
  6.8 8.6 %all-to-all-start = ((bf16[8,256,128]{2,1,0:T(8,128)(2,1)}), bf16[8,256,128]{2,1,0:T(8,128)(2,1)S(1)}, u32[]{:S(2)}, u32[]{:S(2)}) async-start(bf16[8,256,128]{2,1,0:T(8,128)(2,1)} %get-tuple-element.30), calls=%async_computation | async-start | bytes 1048576 | tf_op jit(solution)/shard_map/all_to_all | solution.py:271
  15.5 0.0 collective-permute-done.2
  15.5 0.0 collective-permute-done.1
  15.5 0.0 collective-permute-done
  15.5 3.1 %collective-permute-start.5 = (bf16[4,144,128]{2,1,0:T(8,128)(2,1)S(1)}, bf16[4,144,128]{2,1,0:T(8,128)(2,1)S(1)}, u32[]{:S(2)}, u32[]{:S(2)}) collective-permute-start(bf16[4,144,128]{2,1,0:T(8,128)(2,1)S(1)} %pad_maximum_fusion), channel_id=1, source_target_pairs={{0,192},{8,56},{16,208},{24,8},{32,224},{40,24},{48,240},{56,40},{... | collective-permute-start | bytes 442376 | tf_op jit(solution)/shard_map/ppermute | solution.py:294
  18.6 0.6 collective-permute-start.4
  19.2 1.0 %collective-permute-start.3 = (bf16[4,144,128]{2,1,0:T(8,128)(2,1)S(1)}, bf16[4,144,128]{2,1,0:T(8,128)(2,1)S(1)}, u32[]{:S(2)}, u32[]{:S(2)}) collective-permute-start(bf16[4,144,128]{2,1,0:T(8,128)(2,1)S(1)} %pad_maximum_fusion), channel_id=1, source_target_pairs={{0,64},{8,24},{16,80},{24,40},{32,96},{40,56},{48,112},{56,8},{64,... | collective-permute-start | bytes 442376 | tf_op jit(solution)/shard_map/ppermute | solution.py:294
  20.2 6.6 %collective-permute-done.3 = bf16[4,144,128]{2,1,0:T(8,128)(2,1)S(1)} collective-permute-done((bf16[4,144,128]{2,1,0:T(8,128)(2,1)S(1)}, bf16[4,144,128]{2,1,0:T(8,128)(2,1)S(1)}, u32[]{:S(2)}, u32[]{:S(2)}) %collective-permute-start.3) | collective-permute-done | bytes 147488 | tf_op jit(solution)/shard_map/ppermute | solution.py:294
  26.9 0.0 collective-permute-done.4
  26.9 0.0 collective-permute-done.5
  26.9 0.1 collective-permute-start.6
  27.7 0.7 %broadcast_maximum_fusion.ids_ref = s32[1,1,16]{2,1,0:T(1,128)S(1)} fusion(s32[1,1,16]{2,1,0:T(1,128)} %param.15), kind=kLoop, calls=%fused_computation.8 | loop fusion | flops 16 | bytes 128 | tf_op jit(solution)/shard_map/max | solution.py:322
  28.3 0.7 %collective-permute-done.6.oth_ref = bf16[16,144,128]{2,1,0:T(8,128)(2,1)S(1)} collective-permute-done((bf16[16,144,128]{2,1,0:T(8,128)(2,1)S(1)}, bf16[16,144,128]{2,1,0:T(8,128)(2,1)S(1)}, u32[]{:S(2)}, u32[]{:S(2)}) %collective-permute-start.6) | collective-permute-done | bytes 589856 | tf_op jit(solution)/shard_map/ppermute | solution.py:298
  29.0 1.1 %all-to-all-done.cell_ref.weights_ref = bf16[8,256,128]{2,1,0:T(8,128)(2,1)S(1)} async-done(((bf16[8,256,128]{2,1,0:T(8,128)(2,1)}), bf16[8,256,128]{2,1,0:T(8,128)(2,1)S(1)}, u32[]{:S(2)}, u32[]{:S(2)}) %all-to-all-start) | async-done | bytes 524320 | tf_op jit(solution)/shard_map/all_to_all | solution.py:271
  30.2 4.5 %shard_map.121 = (bf16[8,272,128]{2,1,0:T(8,128)(2,1)}, f32[16,128,128]{2,1,0:T(8,128)S(1)}, bf16[16,128,128]{2,1,0:T(8,128)(2,1)S(1)}) custom-call(s32[1,1,16]{2,1,0:T(1,128)S(1)} %broadcast_maximum_fusion.ids_ref, s32[1,1]{1,0:T(1,128)S(6)} %copy.19.live_ref, bf16[8,256,128]{2,1,0:T(8,128)(2,1)S(1)} %all-to-all-done.cell_ref.weights_ref, ...), custom_call_target="tpu_custom_call" | custom-call | tf_op jit(solution)/shard_map/pallas_call | solution.py:184
  34.7 11.4 %all-to-all-start.1 = ((bf16[8,272,128]{2,1,0:T(8,128)(2,1)}), bf16[8,272,128]{2,1,0:T(8,128)(2,1)S(1)}, u32[]{:S(2)}, u32[]{:S(2)}) async-start(bf16[8,272,128]{2,1,0:T(8,128)(2,1)} %get-tuple-element.41), calls=%async_computation.1 | async-start | bytes 1114112 | tf_op jit(solution)/shard_map/all_to_all | solution.py:271
  46.1 0.1 collective-permute-start.7
  46.2 1.8 %collective-permute-done.7.got_ref = bf16[16,128,128]{2,1,0:T(8,128)(2,1)S(1)} collective-permute-done((bf16[16,128,128]{2,1,0:T(8,128)(2,1)S(1)}, bf16[16,128,128]{2,1,0:T(8,128)(2,1)S(1)}, u32[]{:S(2)}, u32[]{:S(2)}) %collective-permute-start.7) | collective-permute-done | bytes 524320 | tf_op jit(solution)/shard_map/ppermute | solution.py:298
  48.0 0.1 shard_map.122
  48.1 0.7 %collective-permute-start.8 = (bf16[4,128,128]{2,1,0:T(8,128)(2,1)S(1)}, bf16[4,128,128]{2,1,0:T(8,128)(2,1)S(1)}, u32[]{:S(2)}, u32[]{:S(2)}) collective-permute-start(bf16[4,128,128]{2,1,0:T(8,128)(2,1)S(1)} %get-tuple-element.35), channel_id=1, source_target_pairs={{0,16},{8,72},{16,32},{24,88},{32,48},{40,104},{48,0},{56,120},{64... | collective-permute-start | bytes 393224 | tf_op jit(solution)/shard_map/ppermute | solution.py:294
  48.8 0.4 collective-permute-start.9
  49.2 0.9 %collective-permute-start.10 = (bf16[4,128,128]{2,1,0:T(8,128)(2,1)S(1)}, bf16[4,128,128]{2,1,0:T(8,128)(2,1)S(1)}, u32[]{:S(2)}, u32[]{:S(2)}) collective-permute-start(bf16[4,128,128]{2,1,0:T(8,128)(2,1)S(1)} %get-tuple-element.37), channel_id=1, source_target_pairs={{0,48},{8,200},{16,0},{24,216},{32,16},{40,232},{48,32},{56,248},{... | collective-permute-start | bytes 393224 | tf_op jit(solution)/shard_map/ppermute | solution.py:294
  50.2 2.9 %collective-permute-done.8.a_ref = bf16[4,128,128]{2,1,0:T(8,128)(2,1)S(1)} collective-permute-done((bf16[4,128,128]{2,1,0:T(8,128)(2,1)S(1)}, bf16[4,128,128]{2,1,0:T(8,128)(2,1)S(1)}, u32[]{:S(2)}, u32[]{:S(2)}) %collective-permute-start.8) | collective-permute-done | bytes 131104 | tf_op jit(solution)/shard_map/ppermute | solution.py:294
  53.1 2.2 %collective-permute-done.9.b_ref = bf16[4,128,128]{2,1,0:T(8,128)(2,1)S(1)} collective-permute-done((bf16[4,128,128]{2,1,0:T(8,128)(2,1)S(1)}, bf16[4,128,128]{2,1,0:T(8,128)(2,1)S(1)}, u32[]{:S(2)}, u32[]{:S(2)}) %collective-permute-start.9) | collective-permute-done | bytes 131104 | tf_op jit(solution)/shard_map/ppermute | solution.py:294
  55.4 1.3 %collective-permute-done.10.c_ref = bf16[4,128,128]{2,1,0:T(8,128)(2,1)S(1)} collective-permute-done((bf16[4,128,128]{2,1,0:T(8,128)(2,1)S(1)}, bf16[4,128,128]{2,1,0:T(8,128)(2,1)S(1)}, u32[]{:S(2)}, u32[]{:S(2)}) %collective-permute-start.10) | collective-permute-done | bytes 131104 | tf_op jit(solution)/shard_map/ppermute | solution.py:294
  56.7 0.1 shard_map.123
  56.7 1.3 %collective-permute-start.11 = (bf16[128,128]{1,0:T(8,128)(2,1)S(1)}, bf16[128,128]{1,0:T(8,128)(2,1)S(1)}, u32[]{:S(2)}, u32[]{:S(2)}) collective-permute-start(bf16[128,128]{1,0:T(8,128)(2,1)S(1)} %get-tuple-element.38), channel_id=1, source_target_pairs={{0,64},{8,24},{16,80},{24,40},{32,96},{40,56},{48,112},{56,8},{64,... | collective-permute-start | bytes 98312 | tf_op jit(solution)/shard_map/ppermute | solution.py:294
  58.1 0.0 collective-permute-start.12
  58.1 2.8 %collective-permute-start.13 = (bf16[128,128]{1,0:T(8,128)(2,1)S(1)}, bf16[128,128]{1,0:T(8,128)(2,1)S(1)}, u32[]{:S(2)}, u32[]{:S(2)}) collective-permute-start(bf16[128,128]{1,0:T(8,128)(2,1)S(1)} %get-tuple-element.40), channel_id=1, source_target_pairs={{0,192},{8,56},{16,208},{24,8},{32,224},{40,24},{48,240},{56,40},{... | collective-permute-start | bytes 98312 | tf_op jit(solution)/shard_map/ppermute | solution.py:294
  60.8 0.4 all-to-all-done.1.got_ref
  61.3 0.0 copy-done
  61.3 0.8 %shard_map.124 = (f32[256,128]{1,0:T(8,128)}, f32[256,128]{1,0:T(8,128)}) custom-call(bf16[8,272,128]{2,1,0:T(8,128)(2,1)S(1)} %all-to-all-done.1.got_ref, bf16[8,256,128]{2,1,0:T(8,128)(2,1)S(1)} %all-to-all-done.cell_ref.weights_ref, f32[1,256]{1,0:T(1,128)S(1)} %bitcast.12), custom_call_target="tpu_custom_call" | custom-call | tf_op jit(solution)/shard_map/pallas_call | solution.py:275
  62.1 0.0 collective-permute-done.11.a_ref
  62.1 1.4 %collective-permute-done.12.b_ref = bf16[128,128]{1,0:T(8,128)(2,1)S(1)} collective-permute-done((bf16[128,128]{1,0:T(8,128)(2,1)S(1)}, bf16[128,128]{1,0:T(8,128)(2,1)S(1)}, u32[]{:S(2)}, u32[]{:S(2)}) %collective-permute-start.12) | collective-permute-done | bytes 32800 | tf_op jit(solution)/shard_map/ppermute | solution.py:294
  63.5 0.0 collective-permute-done.13.c_ref
  63.5 0.0 copy-done.1
  63.5 0.7 %shard_map.125 = (f32[128,128]{1,0:T(8,128)}, f32[128,128]{1,0:T(8,128)}) custom-call(f32[128,128]{1,0:T(8,128)S(1)} %get-tuple-element.46.keep_ref, bf16[128,128]{1,0:T(8,128)(2,1)S(1)} %collective-permute-done.11.a_ref, bf16[128,128]{1,0:T(8,128)(2,1)S(1)} %collective-permute-done.12.b_ref, bf16[128,128]{1,0:T(8,128)(2,1)S(1)} %collective-permute-done.13.c_ref, ...), custom_call_target="tpu_custom_call" | custom-call | tf_op jit(solution)/shard_map/pallas_call | solution.py:275
  (8 shorter events, 0.1 us)
Async XLA Ops:
  0.6 60.6 %copy-start = (f32[256]{0:T(256)S(1)}, f32[256]{0:T(256)}, u32[]{:S(2)}) copy-start(f32[256]{0:T(256)} %param.11) | copy-start | bytes 3076
  2.7 12.7 %collective-permute-start.2 = (bf16[144,128]{1,0:T(8,128)(2,1)S(1)}, bf16[144,128]{1,0:T(8,128)(2,1)S(1)}, u32[]{:S(2)}, u32[]{:S(2)}) collective-permute-start(bf16[144,128]{1,0:T(8,128)(2,1)S(1)} %get-tuple-element.28.weight_ref), channel_id=1, source_target_pairs={{0,48},{8,200},{16,0},{24,216},{32,16},{40,232},{48,32},{56,248},{... | collective-permute-start | bytes 110600 | tf_op jit(solution)/shard_map/ppermute | solution.py:294
  3.6 11.8 %collective-permute-start.1 = (bf16[144,128]{1,0:T(8,128)(2,1)S(1)}, bf16[144,128]{1,0:T(8,128)(2,1)S(1)}, u32[]{:S(2)}, u32[]{:S(2)}) collective-permute-start(bf16[144,128]{1,0:T(8,128)(2,1)S(1)} %get-tuple-element.28.weight_ref), channel_id=1, source_target_pairs={{0,32},{8,136},{16,48},{24,152},{32,0},{40,168},{48,16},{56,184},{... | collective-permute-start | bytes 110600 | tf_op jit(solution)/shard_map/ppermute | solution.py:294
  6.5 9.0 %collective-permute-start = (bf16[144,128]{1,0:T(8,128)(2,1)S(1)}, bf16[144,128]{1,0:T(8,128)(2,1)S(1)}, u32[]{:S(2)}, u32[]{:S(2)}) collective-permute-start(bf16[144,128]{1,0:T(8,128)(2,1)S(1)} %get-tuple-element.28.weight_ref), channel_id=1, source_target_pairs={{0,16},{8,72},{16,32},{24,88},{32,48},{40,104},{48,0},{56,120},{64... | collective-permute-start | bytes 110600 | tf_op jit(solution)/shard_map/ppermute | solution.py:294
  6.8 56.7 %copy-start.1 = (f32[128]{0:T(128)S(1)}, f32[128]{0:T(128)}, u32[]{:S(2)}) copy-start(f32[128]{0:T(128)} %param.14) | copy-start | bytes 1540
  6.8 23.3 %all-to-all-start = ((bf16[8,256,128]{2,1,0:T(8,128)(2,1)}), bf16[8,256,128]{2,1,0:T(8,128)(2,1)S(1)}, u32[]{:S(2)}, u32[]{:S(2)}) async-start(bf16[8,256,128]{2,1,0:T(8,128)(2,1)} %get-tuple-element.30), calls=%async_computation | async-start | bytes 1048576 | tf_op jit(solution)/shard_map/all_to_all | solution.py:271
  15.5 11.4 %collective-permute-start.5 = (bf16[4,144,128]{2,1,0:T(8,128)(2,1)S(1)}, bf16[4,144,128]{2,1,0:T(8,128)(2,1)S(1)}, u32[]{:S(2)}, u32[]{:S(2)}) collective-permute-start(bf16[4,144,128]{2,1,0:T(8,128)(2,1)S(1)} %pad_maximum_fusion), channel_id=1, source_target_pairs={{0,192},{8,56},{16,208},{24,8},{32,224},{40,24},{48,240},{56,40},{... | collective-permute-start | bytes 442376 | tf_op jit(solution)/shard_map/ppermute | solution.py:294
  18.6 8.3 %collective-permute-start.4 = (bf16[4,144,128]{2,1,0:T(8,128)(2,1)S(1)}, bf16[4,144,128]{2,1,0:T(8,128)(2,1)S(1)}, u32[]{:S(2)}, u32[]{:S(2)}) collective-permute-start(bf16[4,144,128]{2,1,0:T(8,128)(2,1)S(1)} %pad_maximum_fusion), channel_id=1, source_target_pairs={{0,128},{8,40},{16,144},{24,56},{32,160},{40,8},{48,176},{56,24},{... | collective-permute-start | bytes 442376 | tf_op jit(solution)/shard_map/ppermute | solution.py:294
  19.2 7.6 %collective-permute-start.3 = (bf16[4,144,128]{2,1,0:T(8,128)(2,1)S(1)}, bf16[4,144,128]{2,1,0:T(8,128)(2,1)S(1)}, u32[]{:S(2)}, u32[]{:S(2)}) collective-permute-start(bf16[4,144,128]{2,1,0:T(8,128)(2,1)S(1)} %pad_maximum_fusion), channel_id=1, source_target_pairs={{0,64},{8,24},{16,80},{24,40},{32,96},{40,56},{48,112},{56,8},{64,... | collective-permute-start | bytes 442376 | tf_op jit(solution)/shard_map/ppermute | solution.py:294
  26.9 2.1 %collective-permute-start.6 = (bf16[16,144,128]{2,1,0:T(8,128)(2,1)S(1)}, bf16[16,144,128]{2,1,0:T(8,128)(2,1)S(1)}, u32[]{:S(2)}, u32[]{:S(2)}) collective-permute-start(bf16[16,144,128]{2,1,0:T(8,128)(2,1)S(1)} %constant_dynamic-update-slice_fusion.own_ref), channel_id=1, source_target_pairs={{0,8},{8,0},{1,9},{9,1},{2,10},{10,2},{3,11},{11,3},{4,12},{12,4},... | collective-permute-start | bytes 1769480 | tf_op jit(solution)/shard_map/ppermute | solution.py:298
  34.7 26.6 %all-to-all-start.1 = ((bf16[8,272,128]{2,1,0:T(8,128)(2,1)}), bf16[8,272,128]{2,1,0:T(8,128)(2,1)S(1)}, u32[]{:S(2)}, u32[]{:S(2)}) async-start(bf16[8,272,128]{2,1,0:T(8,128)(2,1)} %get-tuple-element.41), calls=%async_computation.1 | async-start | bytes 1114112 | tf_op jit(solution)/shard_map/all_to_all | solution.py:271
  46.1 1.9 %collective-permute-start.7 = (bf16[16,128,128]{2,1,0:T(8,128)(2,1)S(1)}, bf16[16,128,128]{2,1,0:T(8,128)(2,1)S(1)}, u32[]{:S(2)}, u32[]{:S(2)}) collective-permute-start(bf16[16,128,128]{2,1,0:T(8,128)(2,1)S(1)} %get-tuple-element.33), channel_id=1, source_target_pairs={{0,8},{8,0},{1,9},{9,1},{2,10},{10,2},{3,11},{11,3},{4,12},{12,4},... | collective-permute-start | bytes 1572872 | tf_op jit(solution)/shard_map/ppermute | solution.py:298
  48.1 5.0 %collective-permute-start.8 = (bf16[4,128,128]{2,1,0:T(8,128)(2,1)S(1)}, bf16[4,128,128]{2,1,0:T(8,128)(2,1)S(1)}, u32[]{:S(2)}, u32[]{:S(2)}) collective-permute-start(bf16[4,128,128]{2,1,0:T(8,128)(2,1)S(1)} %get-tuple-element.35), channel_id=1, source_target_pairs={{0,16},{8,72},{16,32},{24,88},{32,48},{40,104},{48,0},{56,120},{64... | collective-permute-start | bytes 393224 | tf_op jit(solution)/shard_map/ppermute | solution.py:294
  48.8 6.6 %collective-permute-start.9 = (bf16[4,128,128]{2,1,0:T(8,128)(2,1)S(1)}, bf16[4,128,128]{2,1,0:T(8,128)(2,1)S(1)}, u32[]{:S(2)}, u32[]{:S(2)}) collective-permute-start(bf16[4,128,128]{2,1,0:T(8,128)(2,1)S(1)} %get-tuple-element.36), channel_id=1, source_target_pairs={{0,32},{8,136},{16,48},{24,152},{32,0},{40,168},{48,16},{56,184},{... | collective-permute-start | bytes 393224 | tf_op jit(solution)/shard_map/ppermute | solution.py:294
  49.2 7.4 %collective-permute-start.10 = (bf16[4,128,128]{2,1,0:T(8,128)(2,1)S(1)}, bf16[4,128,128]{2,1,0:T(8,128)(2,1)S(1)}, u32[]{:S(2)}, u32[]{:S(2)}) collective-permute-start(bf16[4,128,128]{2,1,0:T(8,128)(2,1)S(1)} %get-tuple-element.37), channel_id=1, source_target_pairs={{0,48},{8,200},{16,0},{24,216},{32,16},{40,232},{48,32},{56,248},{... | collective-permute-start | bytes 393224 | tf_op jit(solution)/shard_map/ppermute | solution.py:294
  56.7 5.4 %collective-permute-start.11 = (bf16[128,128]{1,0:T(8,128)(2,1)S(1)}, bf16[128,128]{1,0:T(8,128)(2,1)S(1)}, u32[]{:S(2)}, u32[]{:S(2)}) collective-permute-start(bf16[128,128]{1,0:T(8,128)(2,1)S(1)} %get-tuple-element.38), channel_id=1, source_target_pairs={{0,64},{8,24},{16,80},{24,40},{32,96},{40,56},{48,112},{56,8},{64,... | collective-permute-start | bytes 98312 | tf_op jit(solution)/shard_map/ppermute | solution.py:294
  58.1 5.4 %collective-permute-start.12 = (bf16[128,128]{1,0:T(8,128)(2,1)S(1)}, bf16[128,128]{1,0:T(8,128)(2,1)S(1)}, u32[]{:S(2)}, u32[]{:S(2)}) collective-permute-start(bf16[128,128]{1,0:T(8,128)(2,1)S(1)} %get-tuple-element.39), channel_id=1, source_target_pairs={{0,128},{8,40},{16,144},{24,56},{32,160},{40,8},{48,176},{56,24},{... | collective-permute-start | bytes 98312 | tf_op jit(solution)/shard_map/ppermute | solution.py:294
  58.1 5.4 %collective-permute-start.13 = (bf16[128,128]{1,0:T(8,128)(2,1)S(1)}, bf16[128,128]{1,0:T(8,128)(2,1)S(1)}, u32[]{:S(2)}, u32[]{:S(2)}) collective-permute-start(bf16[128,128]{1,0:T(8,128)(2,1)S(1)} %get-tuple-element.40), channel_id=1, source_target_pairs={{0,192},{8,56},{16,208},{24,8},{32,224},{40,24},{48,240},{56,40},{... | collective-permute-start | bytes 98312 | tf_op jit(solution)/shard_map/ppermute | solution.py:294
